TPU v7x, 32 devices: a whole 2x2x4 slice. The times are simulated.
32 devices in a mesh: ctx: 8 (over z, x), head: 4 (over y, core).
Axes of the slice: x: 2, y: 2, z: 4, core: 2. Of those that a mesh axis runs over, the one named last changes fastest.
Arguments:
- queries: bfloat16 [4096, 8192], P('ctx', 'head'), may hold values from -6 to 6
- keys: bfloat16 [4096, 8192], P('ctx', 'head'), may hold values from -6 to 6
- values: bfloat16 [4096, 8192], P('ctx', 'head'), may hold values from -600 to 600
- out_grad: bfloat16 [4096, 6144], P('ctx', 'head'), may hold values from -6 to 6
- out_weight: bfloat16 [6144, 8192], P('ctx', 'head'), may hold values from -0.078125 to 0.078125
- norm_gain: float32 [8192], P('head'), may hold values from 0.1 to 1.9
- slopes: float32 [64], P('head'), may hold values from 0 to 1, as said below
- resp_lengths: int32 [8], replicated, may hold values from 1 to 2048, as said below
Outputs:
- query_grad: bfloat16 [4096, 8192], P('ctx', 'head')
- key_grad: bfloat16 [4096, 8192], P('ctx', 'head')
- value_grad: bfloat16 [4096, 8192], P('ctx', 'head')
Inputs may be any that keep to these rules, and one draw needn't show every extreme that they name: `resp_lengths`: responses are packed in order from position 0 and cover 4096 - 256 / 2 positions; the last 128 positions are padding. The last response is the longest, with 2048 positions. `slopes`: positive decay rates.
All inputs are finite; a program needn't handle non-finite values.
Results may differ from a plain program's by a relative error of at most 0.0063.
Values may be sent and summed in bfloat16 or wider, within the bound.
A program may use at most 192 MiB of HBM per device.

v0:
```python
import jax
import jax.numpy as jnp
from jax import lax
from jax.sharding import PartitionSpec as P

HEADS = 64
DH = 128
BLK = 256
RESP = 8


EPSILON = 1e-06


def entering_2(x, axis, combine, identity, reverse):
    count, position = (lax.axis_size(axis), lax.axis_index(axis))
    everything = jax.tree.map(lambda part: lax.all_gather(part, axis), x)
    start = jax.tree.map(
        lambda part, zero: jnp.broadcast_to(jnp.asarray(zero, part.dtype), part.shape), x, identity
    )

    def hop(k, before):
        at = count - 1 - k if reverse else k
        reached = at > position if reverse else at < position
        new = combine(before, jax.tree.map(lambda part: part[at], everything))
        return jax.tree.map(lambda a, b: jnp.where(reached, a, b), new, before)

    return lax.fori_loop(0, count, hop, start)


def product(form, left, right):
    return jnp.einsum(form, left, right, preferred_element_type=jnp.float32)


def segment_ids(resp_lengths, positions, responses):
    bounds = jnp.cumsum(resp_lengths)
    counted = jnp.sum((positions[:, None] >= bounds[None, :]).astype(jnp.int32), axis=1)
    inside = (counted < responses) & (positions >= 0)
    return jnp.where(inside, counted, -1)


def block_decays(seg_block, slopes):
    places = jnp.arange(seg_block.shape[0], dtype=jnp.float32)
    distance = places[:, None] - places[None, :]
    allowed = (
        (distance >= 0) & (seg_block[:, None] == seg_block[None, :]) & (seg_block[:, None] >= 0)
    )
    decays = jnp.exp(-slopes[:, None, None] * jnp.maximum(distance, 0.0)[None])
    return jnp.where(allowed[None], decays, 0.0)


def state_update(key_state, prev_seg, key_block, value_block, seg_block, slopes):
    block_len = key_block.shape[0]
    places = jnp.arange(block_len, dtype=jnp.float32)
    final_seg = seg_block[block_len - 1]
    tail_mask = ((seg_block == final_seg) & (final_seg >= 0)).astype(jnp.float32)
    factors = jnp.exp(-slopes[None, :] * (block_len - 1.0 - places)[:, None]) * tail_mask[:, None]
    keys_dec = (key_block.astype(jnp.float32) * factors[:, :, None]).astype(jnp.bfloat16)
    carry_mask = ((final_seg == prev_seg) & (final_seg >= 0)).astype(jnp.float32)
    carry_decay = carry_mask * jnp.exp(-slopes * block_len)
    return carry_decay[:, None, None] * key_state + product("thd,the->hde", keys_dec, value_block)


def back_update(grad_state, next_seg, query_block, grad_block, seg_block, slopes):
    block_len = query_block.shape[0]
    places = jnp.arange(block_len, dtype=jnp.float32)
    lead_seg = seg_block[0]
    lead_mask = ((seg_block == lead_seg) & (lead_seg >= 0)).astype(jnp.float32)
    factors = jnp.exp(-slopes[None, :] * places[:, None]) * lead_mask[:, None]
    queries_dec = (query_block.astype(jnp.float32) * factors[:, :, None]).astype(jnp.bfloat16)
    carry_mask = ((lead_seg == next_seg) & (lead_seg >= 0)).astype(jnp.float32)
    carry_decay = carry_mask * jnp.exp(-slopes * block_len)
    return carry_decay[:, None, None] * grad_state + product(
        "thd,the->hde", queries_dec, grad_block
    )


def enter_factors(seg_block, prev_seg, slopes):
    places = jnp.arange(seg_block.shape[0], dtype=jnp.float32)
    enter_mask = ((seg_block == prev_seg) & (seg_block >= 0)).astype(jnp.float32)
    return jnp.exp(-slopes[None, :] * (places[:, None] + 1.0)) * enter_mask[:, None]


def exit_factors(seg_block, next_seg, slopes):
    block_len = seg_block.shape[0]
    places = jnp.arange(block_len, dtype=jnp.float32)
    exit_mask = ((seg_block == next_seg) & (seg_block >= 0)).astype(jnp.float32)
    return jnp.exp(-slopes[None, :] * (block_len - places)[:, None]) * exit_mask[:, None]


def forward_block(carried, inputs, slopes):
    key_state, prev_seg = carried
    query_block, key_block, value_block, seg_block = inputs
    decays = block_decays(seg_block, slopes)
    weights = (product("thd,shd->hts", query_block, key_block) * decays).astype(jnp.bfloat16)
    state_used = key_state.astype(jnp.bfloat16)
    inner = product("hts,shd->thd", weights, value_block)
    outer = product("thd,hde->the", query_block, state_used)
    attended = inner + outer * enter_factors(seg_block, prev_seg, slopes)[:, :, None]
    new_state = state_update(key_state, prev_seg, key_block, value_block, seg_block, slopes)
    return ((new_state, seg_block[seg_block.shape[0] - 1]), (attended, state_used))


def backward_block(carried, inputs, slopes):
    grad_state, next_seg = carried
    query_block, key_block, value_block, grad_block, seg_block, prev_seg, state_used = inputs
    decays = block_decays(seg_block, slopes)
    fwd_weights = (product("thd,shd->hts", query_block, key_block) * decays).astype(jnp.bfloat16)
    back_weights = (product("thd,shd->hts", grad_block, value_block) * decays).astype(jnp.bfloat16)
    back_used = grad_state.astype(jnp.bfloat16)
    entering = enter_factors(seg_block, prev_seg, slopes)[:, :, None]
    leaving = exit_factors(seg_block, next_seg, slopes)[:, :, None]
    query_grad = (
        product("hts,shd->thd", back_weights, key_block)
        + product("the,hde->thd", grad_block, state_used) * entering
    )
    key_grad = (
        product("hts,thd->shd", back_weights, query_block)
        + product("she,hde->shd", value_block, back_used) * leaving
    )
    value_grad = (
        product("hts,the->she", fwd_weights, grad_block)
        + product("shd,hde->she", key_block, back_used) * leaving
    )
    new_state = back_update(grad_state, next_seg, query_block, grad_block, seg_block, slopes)
    return (
        (new_state, seg_block[0]),
        (
            query_grad.astype(jnp.bfloat16),
            key_grad.astype(jnp.bfloat16),
            value_grad.astype(jnp.bfloat16),
        ),
    )


def chain_combine(earlier, latter):
    return (earlier[0] * latter[0], latter[0][:, None, None] * earlier[1] + latter[1])


def per_device(queries, keys, values, out_grad, out_weight, norm_gain, slopes, resp_lengths):
    tokens = queries.shape[0]
    head_count = slopes.shape[0]
    blocks = tokens // BLK
    block_shape = (blocks, BLK, head_count, DH)
    offset = lax.axis_index("ctx") * tokens
    positions = offset + jnp.arange(tokens, dtype=jnp.int32)
    segments = segment_ids(resp_lengths, positions, RESP)
    edges = segment_ids(resp_lengths, jnp.stack([offset - 1, offset + tokens]), RESP)
    before = edges[0]
    beyond = edges[1]
    seg_blocks = segments.reshape(blocks, BLK)
    query_blocks = queries.reshape(block_shape)
    key_blocks = keys.reshape(block_shape)
    value_blocks = values.reshape(block_shape)
    empty = jnp.zeros((head_count, DH, DH), jnp.float32)
    span_decay = jnp.exp(-slopes * tokens)
    total_width = HEADS * DH

    def summary_fwd(carried, inputs):
        key_state, prev_seg = carried
        key_block, value_block, seg_block = inputs
        return (
            (
                state_update(key_state, prev_seg, key_block, value_block, seg_block, slopes),
                seg_block[BLK - 1],
            ),
            None,
        )

    def forward_step(carried, inputs):
        return forward_block(carried, inputs, slopes)

    (local_fwd, _), _ = lax.scan(
        summary_fwd, (empty, before), (key_blocks, value_blocks, seg_blocks)
    )
    link_mask = ((before == segments[tokens - 1]) & (before >= 0)).astype(jnp.float32)
    _, state_in = entering_2(
        (span_decay * link_mask, local_fwd),
        "ctx",
        chain_combine,
        (jnp.ones_like(span_decay), empty),
        False,
    )
    _, (attended, state_used) = lax.scan(
        forward_step, (state_in, before), (query_blocks, key_blocks, value_blocks, seg_blocks)
    )
    attended, state_used = (attended.reshape(tokens, head_count * DH), state_used)
    square_total = lax.psum(jnp.sum(attended * attended, axis=1), "head")
    dy_full = lax.all_gather(out_grad, "head", axis=1, tiled=True)
    gained = norm_gain[None, :] * jnp.dot(
        dy_full,
        lax.all_gather(out_weight, "ctx", axis=0, tiled=True),
        preferred_element_type=jnp.float32,
    )
    cross_total = lax.psum(jnp.sum(attended * gained, axis=1), "head")
    rescale = lax.rsqrt(square_total / total_width + EPSILON)
    cross_mean = cross_total / total_width
    out_delta = jnp.where(
        (segments >= 0)[:, None],
        rescale[:, None] * gained - attended * (rescale**3 * cross_mean)[:, None],
        0.0,
    ).astype(jnp.bfloat16)
    grad_blocks = out_delta.reshape(block_shape)

    def summary_bwd(carried, inputs):
        grad_state, next_seg = carried
        query_block, grad_block, seg_block = inputs
        return (
            (
                back_update(grad_state, next_seg, query_block, grad_block, seg_block, slopes),
                seg_block[0],
            ),
            None,
        )

    (local_bwd, _), _ = lax.scan(
        summary_bwd, (empty, beyond), (query_blocks, grad_blocks, seg_blocks), reverse=True
    )
    back_link = ((beyond == segments[0]) & (beyond >= 0)).astype(jnp.float32)
    _, back_in = entering_2(
        (span_decay * back_link, local_bwd),
        "ctx",
        chain_combine,
        (jnp.ones_like(span_decay), empty),
        True,
    )
    prev_segs = jnp.concatenate([before[None], seg_blocks[:-1, BLK - 1]])

    def backward_step(carried, inputs):
        return backward_block(carried, inputs, slopes)

    _, (query_grad, key_grad, value_grad) = lax.scan(
        backward_step,
        (back_in, beyond),
        (query_blocks, key_blocks, value_blocks, grad_blocks, seg_blocks, prev_segs, state_used),
        reverse=True,
    )
    flat = (tokens, head_count * DH)
    return (query_grad.reshape(flat), key_grad.reshape(flat), value_grad.reshape(flat))


def solution(mesh):
    in_specs = (
        P("ctx", "head"),
        P("ctx", "head"),
        P("ctx", "head"),
        P("ctx", "head"),
        P("ctx", "head"),
        P("head"),
        P("head"),
        P(),
    )
    out_specs = (P("ctx", "head"), P("ctx", "head"), P("ctx", "head"))
    return jax.shard_map(
        per_device, mesh=mesh, in_specs=in_specs, out_specs=out_specs, check_vma=False
    )
```

profile of v0, /device:TPU:0, one launch (start us, length us, event | category | flops | bytes accessed | tf_op | source)
XLA Modules:
  0.0 962.4 jit_solution(3842120112575683733)
XLA Ops:
  14.5 2.9 copy.78
  21.7 10.3 %while.106 = (s32[]{:T(128)}, f32[16,128,128]{2,1,0:T(8,128)S(1)}, s32[]{:T(128)}, s32[2,256]{1,0:T(2,128)S(1)}, f32[16,1,1]{0,2,1:T(1,128)S(1)}, /*index=5*/bf1...) while((s32[]{:T(128)}, f32[16,128,128]{2,1,0:T(8,128)S(1)}, ...), condition=%wide.region_4.5_spmd.clone, body=%wide.region_3.4_spmd.clone.sunk | while | flops 136586272 | bytes 4234110 | solution.py:173
  37.8 23.9 %all-reduce.2 = (f32[128]{0:T(128)S(1)}, f32[128]{0:T(128)S(1)}) all-reduce(f32[128]{0:T(128)S(1)} %multiply_dynamic-update-slice_fusion.1, f32[128]{0:T(128)S(1)} %get-tuple-element.1343), channel_id=2, replica_groups=mesh['ctx'=8,'head'=4] {'ctx'}, use_global_device_ids=true, to_apply=%add | all-reduce | flops 256 | bytes 2048
  61.8 3.6 copy.110
  65.4 4.3 copy.84
  69.7 91.3 %all-gather.13.cloned.1.call-done = f32[128,128,128]{2,1,0:T(8,128)} async-done(((f32[16,128,128]{2,1,0:T(8,128)}), f32[128,128,128]{2,1,0:T(8,128)}) %all-gather.13.cloned.1.call-update) | async-done | bytes 8388624 | tf_op jit(solution)/shard_map/all_gather | solution.py:17
  160.9 12.5 %while.107 = (s32[]{:T(128)}, f32[16,128,128]{2,1,0:T(8,128)S(1)}, s32[]{:T(128)}, f32[8,16]{1,0:T(8,128)S(1)}, f32[8,16,128,128]{3,2,1,0:T(8,128)}, /*index=5*/s32[]{:T(128)}, s32[]{:T(128)}) while((s32[]{:T(128)}, f32[16,128,128]{2,1,0:T(8,128)S(1)}, s32[]{:T(128)}, f32[8,16]{1,0:T(8,128)S(1)}, f32[8,16,128,128]{3,2,1,0:T(8,128)}, ...), condition=%wide.region_6.7_spmd.clone, body=%wide.region_5.6_spmd.clone.sunk | while | flops 1048580 | bytes 3146025 | solution.py:28
  173.4 37.0 %while.104 = (s32[]{:T(128)}, f32[16,128,128]{2,1,0:T(8,128)S(1)}, s32[]{:T(128)}, f32[2,256,16,128]{1,3,2,0:T(8,128)}, bf16[2,16,128,128]{3,2,1,0:T(8,128)(2,1)...) while((s32[]{:T(128)}, f32[16,128,128]{2,1,0:T(8,128)S(1)}, ...), condition=%wide.region_8.9_spmd, body=%wide.region_7.8_spmd.sunk | while | flops 813648128 | bytes 26426296 | solution.py:184
  175.4 3.3 constant_dynamic-slice_fusion.12
  178.7 4.7 fusion.146
  183.5 3.8 bitcast_dynamic-update-slice_fusion.4
  193.9 3.3 constant_dynamic-slice_fusion.12
  197.2 4.8 fusion.146
  202.1 3.8 bitcast_dynamic-update-slice_fusion.4
  210.5 5.5 copy.83
  215.9 2.9 multiply_reduce_fusion
  218.9 470.2 %all-gather.11.cloned.1.call-done = bf16[6144,2048]{1,0:T(8,128)(2,1)} async-done(((bf16[768,2048]{1,0:T(8,128)(2,1)}), bf16[6144,2048]{1,0:T(8,128)(2,1)}) %all-gather.11.cloned.1.call-update) | async-done | bytes 25165840 | tf_op jit(solution)/shard_map/all_gather | solution.py:192
  689.1 22.6 %fusion.92 = (f32[512]{0:T(512)S(1)}, f32[512,2048]{1,0:T(8,128)}) fusion(f32[64,8,16,128]{3,2,1,0:T(8,128)} %bitcast.346, f32[2048]{0:T(1024)S(1)} %copy-done.13, bf16[512,6144]{1,0:T(8,128)(2,1)} %all-gather.9.cloned.1.call-done, bf16[6144,2048]{1,0:T(8,128)(2,1)} %all-gather.11.cloned.1.call-done), kind=kOutput, calls=%fused_computation.149 | convolution fusion | flops 12888047616 | bytes 39856128 | tf_op jit(solution)/shard_map/dot_general | solution.py:190
  711.7 7.1 all-reduce.3
  718.8 4.8 fusion.96
  726.1 10.7 %while.108 = (s32[]{:T(128)}, f32[16,128,128]{2,1,0:T(8,128)S(1)}, s32[]{:T(128)}, s32[2,256]{1,0:T(2,128)S(1)}, f32[16,1,1]{0,2,1:T(1,128)S(1)}, /*index=5*/bf1...) while((s32[]{:T(128)}, f32[16,128,128]{2,1,0:T(8,128)S(1)}, ...), condition=%wide.region_14.15_spmd.clone, body=%wide.region_13.14_spmd.clone.sunk | while | flops 136586016 | bytes 4232117 | solution.py:216
  739.8 122.1 %all-gather.15.cloned.1.call-done = f32[128,128,128]{2,1,0:T(8,128)} async-done(((f32[16,128,128]{2,1,0:T(8,128)}), f32[128,128,128]{2,1,0:T(8,128)}) %all-gather.15.cloned.1.call-update) | async-done | bytes 8388624 | tf_op jit(solution)/shard_map/all_gather | solution.py:17
  861.9 12.0 %while.109 = (s32[]{:T(128)}, f32[16,128,128]{2,1,0:T(8,128)S(1)}, s32[]{:T(128)}, f32[8,16]{1,0:T(8,128)S(1)}, f32[8,16,128,128]{3,2,1,0:T(8,128)}, /*index=5*/s32[]{:T(128)}, s32[]{:T(128)}, s32[]{:T(128)}, s32[]{:T(128)}) while((s32[]{:T(128)}, f32[16,128,128]{2,1,0:T(8,128)S(1)}, s32[]{:T(128)}, f32[8,16]{1,0:T(8,128)S(1)}, ...), condition=%wide.region_16.17_spmd.clone, body=%wide.region_15.16_spmd.clone.sunk | while | flops 1048584 | bytes 3146087 | solution.py:28
  878.8 69.3 %while.105 = (s32[]{:T(128)}, f32[16,128,128]{2,1,0:T(8,128)S(1)}, s32[]{:T(128)}, bf16[2,256,16,128]{3,2,1,0:T(8,128)(2,1)}, bf16[2,256,16,128]{3,2,1,0:T(8,128...) while((s32[]{:T(128)}, f32[16,128,128]{2,1,0:T(8,128)S(1)}, ...), condition=%wide.region_18.19_spmd, body=%wide.region_17.18_spmd.sunk | while | flops 1895263232 | bytes 99159848 | solution.py:232
  891.3 4.9 fusion.167
  896.2 3.5 fusion.168
  902.3 3.4 constant_dynamic-update-slice_fusion.6
  925.8 4.9 fusion.167
  930.6 3.5 fusion.168
  936.7 3.4 constant_dynamic-update-slice_fusion.6
  948.1 3.6 copy.136
  951.7 4.1 copy_bitcast_fusion.8
  (205 shorter events, 109.7 us)
Async XLA Ops:
  7.2 153.8 %all-gather.13.cloned.1.call-start = ((), (), s32[]{:S(2)}) async-start(), calls=%async_computation.2 | async-start | bytes 9437184 | tf_op jit(solution)/shard_map/all_gather | solution.py:17
  14.5 2.9 copy-start.6
  19.7 0.7 copy-start.15
  19.7 1.9 copy-start.14
  31.9 1.0 copy-start.9
  33.0 186.0 %all-gather.9.cloned.1.call-start = ((), (), s32[]{:S(2)}) async-start(), calls=%async_computation | async-start | bytes 7864320 | tf_op jit(solution)/shard_map/all_gather | solution.py:189
  33.7 655.4 %all-gather.11.cloned.1.call-start = ((), (), s32[]{:S(2)}) async-start(), calls=%async_computation.1 | async-start | bytes 28311552 | tf_op jit(solution)/shard_map/all_gather | solution.py:192
  34.4 827.5 %all-gather.15.cloned.1.call-start = ((), (), s32[]{:S(2)}) async-start(), calls=%async_computation.3 | async-start | bytes 9437184 | tf_op jit(solution)/shard_map/all_gather | solution.py:17
  187.9 1.4 copy-start.5
  206.5 1.4 copy-start.5
  215.9 473.2 %copy-start.13 = (f32[2048]{0:T(1024)S(1)}, f32[2048]{0:T(1024)}, u32[]{:S(2)}) copy-start(f32[2048]{0:T(1024)} %param.25) | copy-start | bytes 24580
  724.2 1.9 copy-start.7
  736.8 1.0 copy-start.8
  878.8 3.9 copy-start
  882.8 2.7 copy-start.2
  902.3 3.4 copy-start.4
  905.6 1.6 copy-start.3
  905.6 1.9 copy-start.12
  910.8 2.4 copy-start.1
  913.2 3.9 copy-start
  917.2 2.7 copy-start.2
  936.7 3.4 copy-start.4
  940.2 1.6 copy-start.3
  940.2 1.9 copy-start.12
  945.4 2.4 copy-start.1
  948.1 3.6 copy-start.10
  948.1 3.6 copy-start.11
Sparse Core Ops, SparseCore 0:
  33.1 127.8 all-gather.12
  162.5 44.5 all-gather.8
  208.6 480.4 all-gather.10
  737.9 123.9 all-gather.14
where the time goes:
time: 964 us; the launch traced here: 962 us
  waiting for transfers between devices  685 us (71%)
  matrix products  87 us (9%)
  local copies, waits for them, and re-layouts  78.5 us (8%)
  other arithmetic  44 us (5%)
  blocking collectives  31 us (3%)
  between operations  20.4 us (2%)
  loops' own time  16.2 us (2%)
    all_gather x1, waiting for transfers between devices, per_device(): lax.all_gather(out_weight, 'ctx', axis=0, tiled=True)  470 us
    all_gather x2, waiting for transfers between devices, entering_2(): everything = jax.tree.map(lambda part: lax.all_gather(part, axis), x)  213 us
    dot_general x26, matrix products, product(): return jnp.einsum(form, left, right, preferred_element_type=jnp.float32)  64.4 us
    unnamed x31, local copies, waits for them, and re-layouts  24.5 us
    unnamed x1, blocking collectives  23.9 us
    select_n x16, other arithmetic, hop(): return jax.tree.map(lambda a, b: jnp.where(reached, a, b), new, before)  23.9 us
    dot_general x1, matrix products, per_device(): jnp.dot(dy_full, lax.all_gather(out_weight, 'ctx', axis=0, tiled=True), p...  22.6 us
    dynamic_update_slice x10, local copies, waits for them, and re-layouts, per_device(): lax.scan(backward_step, (back_in, beyond), (query_blocks, key_blocks, val...  21.8 us
  transfers between devices with their start and end apart: 4, of which 3 were waited for; matrix products, arithmetic and copies ran while one was open for 7% of the time, Pallas kernels for 0%

commit v1 on v0

v1 whole, which is shorter than its diff:
```python
import jax
import jax.numpy as jnp
from jax import lax
from jax.experimental import pallas as pl
from jax.experimental.pallas import tpu as pltpu
from jax.sharding import PartitionSpec as P

HEADS = 64
DH = 128
BLK = 256
RESP = 8
EPSILON = 1e-06
VMEM_BYTES = 40 * 1024 * 1024

ENTER, EXIT, TAIL, LEAD, SCALE, CROSS = range(6)


def segment_ids(resp_lengths, positions, responses):
    bounds = jnp.cumsum(resp_lengths)
    counted = jnp.sum((positions[:, None] >= bounds[None, :]).astype(jnp.int32), axis=1)
    inside = (counted < responses) & (positions >= 0)
    return jnp.where(inside, counted, -1)


def dot(left, right, left_dim, right_dim):
    return lax.dot_general(
        left, right, (((left_dim,), (right_dim,)), ((), ())), preferred_element_type=jnp.float32
    )


def places():
    return lax.broadcasted_iota(jnp.int32, (BLK, 1), 0).astype(jnp.float32)


def tile_exp(slope, steps):
    return jnp.exp(jnp.full((1, DH), -slope * steps, jnp.float32))


def decays_of(seg_col, seg_row, slope):
    shape = (BLK, BLK)
    distance = lax.broadcasted_iota(jnp.int32, shape, 0) - lax.broadcasted_iota(jnp.int32, shape, 1)
    allowed = (distance >= 0) & (seg_col == seg_row) & (seg_col >= 0)
    faded = jnp.exp(-slope * jnp.maximum(distance, 0).astype(jnp.float32))
    return jnp.where(allowed, faded, 0.0)


def blocks_of(ref):
    return ref.shape[0] // BLK


def rows(b):
    return pl.ds(b * BLK, BLK)


def weighted(coef_ref, gathered_ref, head):
    total = jnp.zeros((DH, DH), jnp.float32)
    for j in range(gathered_ref.shape[0]):
        total += coef_ref[j, head] * gathered_ref[j, 0].astype(jnp.float32)
    return total


def next_state(state, k, v, table, slope, carry):
    faded = jnp.exp(-slope * (BLK - 1.0 - places())) * table[:, TAIL : TAIL + 1]
    update = dot((k.astype(jnp.float32) * faded).astype(jnp.bfloat16), v, 0, 0)
    if state is None:
        return update
    return (carry * tile_exp(slope, BLK)) * state + update


def summary_kernel(slopes, carries, k_ref, v_ref, table_ref, out_ref):
    slope = slopes[pl.program_id(0)]
    state = None
    for b in range(blocks_of(k_ref)):
        state = next_state(
            state, k_ref[rows(b), :], v_ref[rows(b), :], table_ref[rows(b), :], slope, carries[0, b]
        )
    out_ref[0] = state.astype(out_ref.dtype)


def forward_kernel(
    slopes, carries, coef_ref, gathered_ref, q_ref, k_ref, v_ref, table_ref, col_ref, row_ref,
    attended_ref, used_ref,
):
    head = pl.program_id(0)
    slope = slopes[head]
    state = weighted(coef_ref, gathered_ref, head)
    for b in range(blocks_of(q_ref)):
        q, k, v = q_ref[rows(b), :], k_ref[rows(b), :], v_ref[rows(b), :]
        table = table_ref[rows(b), :]
        decays = decays_of(col_ref[rows(b), :], row_ref[:, rows(b)], slope)
        weights = (dot(q, k, 1, 1) * decays).astype(jnp.bfloat16)
        used = state.astype(jnp.bfloat16)
        used_ref[b, 0] = used
        entering = jnp.exp(-slope * (places() + 1.0)) * table[:, ENTER : ENTER + 1]
        attended_ref[rows(b), :] = dot(weights, v, 1, 0) + entering * dot(q, used, 1, 0)
        state = next_state(state, k, v, table, slope, carries[0, b])


def backward_kernel(
    slopes, carries, q_ref, k_ref, v_ref, gained_ref, attended_ref, used_ref, table_ref, col_ref,
    row_ref, dq_ref, dk_ref, dv_ref, local_ref, total_ref,
):
    slope = slopes[pl.program_id(0)]
    state = jnp.zeros((DH, DH), jnp.float32)
    for b in reversed(range(blocks_of(q_ref))):
        q, k, v = q_ref[rows(b), :], k_ref[rows(b), :], v_ref[rows(b), :]
        table = table_ref[rows(b), :]
        delta = (
            table[:, SCALE : SCALE + 1] * gained_ref[rows(b), :]
            - table[:, CROSS : CROSS + 1] * attended_ref[rows(b), :]
        ).astype(jnp.bfloat16)
        decays = decays_of(col_ref[rows(b), :], row_ref[:, rows(b)], slope)
        fwd_weights = (dot(q, k, 1, 1) * decays).astype(jnp.bfloat16)
        back_weights = (dot(delta, v, 1, 1) * decays).astype(jnp.bfloat16)
        entering = jnp.exp(-slope * (places() + 1.0)) * table[:, ENTER : ENTER + 1]
        dq = dot(back_weights, k, 1, 0) + entering * dot(delta, used_ref[b, 0], 1, 1)
        dq_ref[rows(b), :] = dq.astype(dq_ref.dtype)
        dk_ref[rows(b), :] = dot(back_weights, q, 0, 0)
        dv_ref[rows(b), :] = dot(fwd_weights, delta, 0, 0)
        local_ref[b, 0] = state
        leading = jnp.exp(-slope * places()) * table[:, LEAD : LEAD + 1]
        faded = (q.astype(jnp.float32) * leading).astype(jnp.bfloat16)
        state = (carries[1, b] * tile_exp(slope, BLK)) * state + dot(faded, delta, 0, 0)
    total_ref[0] = state.astype(total_ref.dtype)


def finish_kernel(
    slopes, carries, coef_ref, gathered_ref, k_ref, v_ref, local_ref, table_ref, dk_ref, dv_ref,
    dk_out, dv_out,
):
    head = pl.program_id(0)
    slope = slopes[head]
    entering = weighted(coef_ref, gathered_ref, head)
    count = blocks_of(k_ref)
    for b in range(count):
        reach = carries[2, b] * tile_exp(slope, BLK * (count - 1 - b))
        used = (local_ref[b, 0] + reach * entering).astype(jnp.bfloat16)
        leaving = jnp.exp(-slope * (BLK - places())) * table_ref[rows(b), EXIT : EXIT + 1]
        dk = dk_ref[rows(b), :] + leaving * dot(v_ref[rows(b), :], used, 1, 1)
        dv = dv_ref[rows(b), :] + leaving * dot(k_ref[rows(b), :], used, 1, 0)
        dk_out[rows(b), :] = dk.astype(dk_out.dtype)
        dv_out[rows(b), :] = dv.astype(dv_out.dtype)


def smem():
    return pl.BlockSpec(memory_space=pltpu.SMEM)


def columns(tokens):
    return pl.BlockSpec((tokens, DH), lambda h: (0, h))


def whole(shape):
    return pl.BlockSpec(shape, lambda h: (0,) * len(shape))


def stack(count):
    return pl.BlockSpec((count, 1, DH, DH), lambda h: (0, h, 0, 0))


def one_state():
    return pl.BlockSpec((1, DH, DH), lambda h: (h, 0, 0))


def call(kernel, heads, in_specs, out_specs, out_shape, operands, flops, moved):
    return pl.pallas_call(
        kernel,
        grid=(heads,),
        in_specs=in_specs,
        out_specs=out_specs,
        out_shape=out_shape,
        compiler_params=pltpu.CompilerParams(vmem_limit_bytes=VMEM_BYTES),
        cost_estimate=pl.CostEstimate(flops=flops, bytes_accessed=moved, transcendentals=0),
    )(*operands)


def ring_order(count):
    return [*range(0, count, 2), *range(count - 1 - count % 2, 0, -2)]


def ring_matmul(dy, weight, count):
    order = ring_order(count)
    table = jnp.asarray(order, jnp.int32)
    spot = [order.index(i) for i in range(count)]
    position = jnp.asarray(spot, jnp.int32)[lax.axis_index("ctx")]
    up = [(order[i], order[(i + 1) % count]) for i in range(count)]
    down = [(b, a) for a, b in up]
    depth = weight.shape[0]
    width = dy.shape[2]

    def term(block, step, low):
        owner = table[lax.rem(position + step + count, count)]
        start = owner * depth + low
        part = lax.dynamic_slice(
            dy, (start // width, 0, lax.rem(start, width)), (1, dy.shape[1], block.shape[0])
        )[0]
        return jnp.dot(part, block, preferred_element_type=jnp.float32)

    total = term(weight, 0, 0)
    from_left = from_right = weight
    for step in range(1, (count - 1) // 2 + 1):
        from_left = lax.ppermute(from_left, "ctx", up)
        from_right = lax.ppermute(from_right, "ctx", down)
        total = total + term(from_left, -step, 0)
        total = total + term(from_right, step, 0)
    if count % 2 == 0:
        half = depth // 2
        left = lax.ppermute(from_left[:half], "ctx", up)
        right = lax.ppermute(from_right[half:], "ctx", down)
        total = total + term(left, -(count // 2), 0)
        total = total + term(right, count // 2, half)
    return total


def per_device(queries, keys, values, out_grad, out_weight, norm_gain, slopes, resp_lengths):
    tokens = queries.shape[0]
    heads = slopes.shape[0]
    blocks = tokens // BLK
    width = heads * DH
    count = lax.axis_size("ctx")
    me = lax.axis_index("ctx")
    offset = me * tokens
    positions = offset - 1 + jnp.arange(tokens + 2, dtype=jnp.int32)
    padded = segment_ids(resp_lengths, positions, RESP)
    segments, before, beyond = padded[1:-1], padded[0], padded[-1]
    firsts = segments[::BLK]
    lasts = segments[BLK - 1 :: BLK]
    prevs = jnp.concatenate([before[None], lasts[:-1]])
    nexts = jnp.concatenate([firsts[1:], beyond[None]])

    def spread(per_block):
        return jnp.repeat(per_block, BLK)

    def linked(left, right):
        return ((left == right) & (left >= 0)).astype(jnp.float32)

    masks = [linked(segments, spread(x)) for x in (prevs, nexts, lasts, firsts)]
    valid = (segments >= 0).astype(jnp.float32)
    reach = linked(nexts, jnp.broadcast_to(beyond, nexts.shape)).at[blocks - 1].set(1.0)
    carries = jnp.stack([linked(lasts, prevs), linked(firsts, nexts), reach])
    table = jnp.stack(masks + [valid, valid], axis=1)
    seg_col, seg_row = segments[:, None], segments[None, :]

    spans = jnp.arange(count, dtype=jnp.int32)
    ends = segment_ids(resp_lengths, spans * tokens + (tokens - 1), RESP)
    starts = segment_ids(resp_lengths, spans * tokens, RESP)

    def coefficients(hops, same):
        faded = jnp.exp(-slopes[None, :] * (jnp.maximum(hops, 0) * tokens)[:, None].astype(jnp.float32))
        return jnp.where(((hops >= 0) & same)[:, None], faded, 0.0)

    fwd_coef = coefficients(me - 1 - spans, ends == before)
    bwd_coef = coefficients(spans - me - 1, starts == beyond)

    f32, bf16 = jnp.float32, jnp.bfloat16
    sheet = lambda kind: jax.ShapeDtypeStruct((tokens, width), kind)
    states = jax.ShapeDtypeStruct((heads, DH, DH), bf16)
    per_head = lambda kind: jax.ShapeDtypeStruct((blocks, heads, DH, DH), kind)
    col, table_spec = columns(tokens), whole((tokens, 6))
    seg_specs = [whole((tokens, 1)), whole((1, tokens))]
    unit = 2 * tokens * BLK * width
    size = 2 * tokens * width

    local = call(
        summary_kernel, heads, [smem(), smem(), col, col, table_spec], one_state(), states,
        (slopes, carries, keys, values, table), unit // 2, 2 * size,
    )
    gathered = lax.all_gather(local, "ctx")
    dy = lax.all_gather(out_grad, "head")
    norm_grad = ring_matmul(dy, out_weight, count)

    attended, used = call(
        forward_kernel, heads,
        [smem(), smem(), smem(), stack(count), col, col, col, table_spec, *seg_specs],
        (col, stack(blocks)), (sheet(f32), per_head(bf16)),
        (slopes, carries, fwd_coef, gathered, queries, keys, values, table, seg_col, seg_row),
        3 * unit, 9 * size,
    )
    square_total = lax.psum(jnp.sum(attended * attended, axis=1), "head")
    rescale = lax.rsqrt(square_total / (HEADS * DH) + EPSILON)
    gained = norm_gain[None, :] * norm_grad
    cross_total = lax.psum(jnp.sum(attended * gained, axis=1), "head")
    cross_mean = cross_total / (HEADS * DH)
    back_table = jnp.stack(masks + [valid * rescale, valid * rescale**3 * cross_mean], axis=1)

    dq, dk, dv, inner, total = call(
        backward_kernel, heads,
        [smem(), smem(), col, col, col, col, col, stack(blocks), table_spec, *seg_specs],
        (col, col, col, stack(blocks), one_state()),
        (sheet(bf16), sheet(f32), sheet(f32), per_head(f32), states),
        (slopes, carries, queries, keys, values, gained, attended, used, back_table, seg_col, seg_row),
        6 * unit, 12 * size,
    )
    back_gathered = lax.all_gather(total, "ctx")
    dk, dv = call(
        finish_kernel, heads,
        [smem(), smem(), smem(), stack(count), col, col, stack(blocks), table_spec, col, col],
        (col, col), (sheet(bf16), sheet(bf16)),
        (slopes, carries, bwd_coef, back_gathered, keys, values, inner, table, dk, dv),
        unit, 10 * size,
    )
    return dq, dk, dv


def solution(mesh):
    split = P("ctx", "head")
    return jax.shard_map(
        per_device,
        mesh=mesh,
        in_specs=(split, split, split, split, split, P("head"), P("head"), P()),
        out_specs=(split, split, split),
        check_vma=False,
    )
```

time: 964 us -> 493 us (0.51)
  waiting for transfers between devices: 685 us -> 293 us
  Pallas kernels: 0 us -> 58.4 us
  local copies, waits for them, and re-layouts: 78.5 us -> 30.3 us
  other arithmetic: 44 us -> 6.79 us
  blocking collectives: 31 us -> 5.64 us
  matrix products: 87 us -> 62.2 us
  loops' own time: 16.2 us -> 0 us
    all_gather x4 -> x3, waiting for transfers between devices: 684 us -> 74.6 us  [the longest x1 74.6 us: per_device(): back_gathered = lax.all_gather(total, 'ctx')]
    ppermute x0 -> x8, waiting for transfers between devices: none -> 218 us  [the longest x3 218 us: ring_matmul(): from_right = lax.ppermute(from_right, 'ctx', down)]
    pallas_call x0 -> x4, Pallas kernels: none -> 58.4 us  [call(): pl.pallas_call(kernel, grid=(heads,), in_specs=in_specs, out_specs=out_sp...]
    dot_general x27 -> x9, matrix products: 87 us -> 62.2 us  [term(): return jnp.dot(part, block, preferred_element_type=jnp.float32)]
    unnamed x1 -> x0, blocking collectives: 23.9 us -> none
    select_n x16 -> x1, other arithmetic: 23.9 us -> 0.08 us  [coefficients(): return jnp.where(((hops >= 0) & same)[:, None], faded, 0.0)]
    dynamic_update_slice x10 -> x0, local copies, waits for them, and re-layouts: 21.8 us -> none  [per_device(): lax.scan(backward_step, (back_in, beyond), (query_blocks, key_blocks, val...]
    another operation x6 -> x0, loops' own time: 16.2 us -> none  [the longest x1 4.32 us: per_device(): lax.scan(backward_step, (back_in, beyond), (query_blocks, key_blocks, val...]
  transfers between devices with their start and end apart: 4 -> 11, of which waited for: 3 -> 5; matrix products, arithmetic and copies ran while one was open for 7% -> 10% of each run, Pallas kernels for 0% -> 3%
where the time goes in v1:
time: 493 us; the launch traced here: 491 us
  waiting for transfers between devices  293 us (59%)
  matrix products  62.2 us (13%)
  Pallas kernels  58.4 us (12%)
  local copies, waits for them, and re-layouts  30.3 us (6%)
  between operations  26.3 us (5%)
  starting transfers between devices  9.07 us (2%)
  other arithmetic  6.79 us (1%)
  blocking collectives  5.64 us (1%)
    ppermute x3, waiting for transfers between devices, ring_matmul(): from_right = lax.ppermute(from_right, 'ctx', down)  218 us
    all_gather x1, waiting for transfers between devices, per_device(): back_gathered = lax.all_gather(total, 'ctx')  74.6 us
    dot_general x9, matrix products, term(): return jnp.dot(part, block, preferred_element_type=jnp.float32)  62.2 us
    pallas_call x4, Pallas kernels, call(): pl.pallas_call(kernel, grid=(heads,), in_specs=in_specs, out_specs=out_sp...  58.4 us
    unnamed x50, local copies, waits for them, and re-layouts  21.4 us
  transfers between devices with their start and end apart: 11, of which 5 were waited for; matrix products, arithmetic and copies ran while one was open for 10% of the time, Pallas kernels for 3%

profile of v1, /device:TPU:0, one launch (start us, length us, event | category | flops | bytes accessed | tf_op | source)
XLA Modules:
  0.0 491.5 jit_solution(14474039261218071666)
XLA Ops:
  9.8 2.0 fusion.41
  12.3 2.0 and_convert_fusion.4
  16.0 1.6 copy-done.2
  18.3 9.3 %shard_map.121 = bf16[16,128,128]{2,1,0:T(8,128)(2,1)} custom-call(f32[16]{0:T(128)S(1)} %copy-done.15, f32[3,2]{1,0:T(4,128)S(1)} %pad_maximum_fusion.carries, bf16[512,2048]{1,0:T(8,128)(2,1)S(1)} %copy-done, bf16[512,2048]{1,0:T(8,128)(2,1)S(1)} %copy-done.2, f32[512,6]{1,0:T(8,128)S(1)} %copy.33.table_ref), custom_call_target="tpu_custom_call" | custom-call | flops 268435456 | bytes 4194304 | tf_op jit(solution)/shard_map/pallas_call | solution.py:166
  27.7 3.0 collective-permute-start.1
  30.9 118.8 %collective-permute-done.1 = bf16[768,2048]{1,0:T(8,128)(2,1)} collective-permute-done((bf16[768,2048]{1,0:T(8,128)(2,1)}, bf16[768,2048]{1,0:T(8,128)(2,1)}, u32[]{:S(2)}, u32[]{:S(2)}) %collective-permute-start.1) | collective-permute-done | bytes 3145760 | tf_op jit(solution)/shard_map/ppermute | solution.py:203
  151.8 67.6 %collective-permute-done.3 = bf16[768,2048]{1,0:T(8,128)(2,1)} collective-permute-done((bf16[768,2048]{1,0:T(8,128)(2,1)}, bf16[768,2048]{1,0:T(8,128)(2,1)}, u32[]{:S(2)}, u32[]{:S(2)}) %collective-permute-start.3) | collective-permute-done | bytes 3145760 | tf_op jit(solution)/shard_map/ppermute | solution.py:203
  238.5 1.6 copy-done.8
  240.1 13.5 %shard_map.122 = (f32[512,2048]{1,0:T(8,128)S(1)}, bf16[2,16,128,128]{3,2,1,0:T(8,128)(2,1)S(1)}) custom-call(f32[16]{0:T(128)S(1)} %copy-done.16, f32[3,2]{1,0:T(4,128)S(1)} %pad_maximum_fusion.carries, f32[8,16]{1,0:T(8,128)S(1)} %get-tuple-element.54.coef_ref, bf16[8,16,128,128]{3,2,1,0:T(8,128)(2,1)} %bitcast.115, bf16[512,2048]{1,0:T(8,128)(2,1)S(1)} %copy-done.8, ...), custom_call_target="tpu_custom_call" | custom-call | flops 1610612736 | bytes 18874368 | tf_op jit(solution)/shard_map/pallas_call | solution.py:166
  253.6 2.0 copy-done.6
  256.6 31.4 %collective-permute-done.5 = bf16[768,2048]{1,0:T(8,128)(2,1)} collective-permute-done((bf16[768,2048]{1,0:T(8,128)(2,1)}, bf16[768,2048]{1,0:T(8,128)(2,1)}, u32[]{:S(2)}, u32[]{:S(2)}) %collective-permute-start.5) | collective-permute-done | bytes 3145760 | tf_op jit(solution)/shard_map/ppermute | solution.py:203
  288.0 2.7 slice.47
  291.0 2.7 slice.46
  293.8 1.7 collective-permute-start.6
  295.5 6.2 %fusion.14 = f32[512,2048]{1,0:T(8,128)} fusion(bf16[768,2048]{1,0:T(8,128)(2,1)} %param.16, bf16[4,512,1536]{2,1,0:T(8,128)(2,1)} %bitcast.116, s32[]{:T(128)S(6)} %select_n.143, s32[]{:T(128)S(6)} %select_n.144), kind=kOutput, calls=%fused_computation.15 | convolution fusion | flops 1610612736 | bytes 8126472 | tf_op jit(solution)/shard_map/dot_general | solution.py:197
  301.7 5.8 %fusion.4 = f32[512,2048]{1,0:T(8,128)} fusion(bf16[768,2048]{1,0:T(8,128)(2,1)} %collective-permute-done.4, bf16[4,512,1536]{2,1,0:T(8,128)(2,1)S(1)} %bitcast.118, s32[]{:T(128)S(6)} %select_n.163, s32[]{:T(128)S(6)} %select_n.164), kind=kOutput, calls=%fused_computation.5 | convolution fusion | flops 1610612736 | bytes 8126472 | tf_op jit(solution)/shard_map/dot_general | solution.py:197
  307.4 5.7 %fusion.8 = f32[512,2048]{1,0:T(8,128)} fusion(bf16[768,2048]{1,0:T(8,128)(2,1)} %collective-permute-done.2, bf16[4,512,1536]{2,1,0:T(8,128)(2,1)S(1)} %bitcast.119, s32[]{:T(128)S(6)} %select_n.155, s32[]{:T(128)S(6)} %select_n.156), kind=kOutput, calls=%fused_computation.9 | convolution fusion | flops 1610612736 | bytes 8126472 | tf_op jit(solution)/shard_map/dot_general | solution.py:197
  313.2 5.8 %fusion.12 = f32[512,2048]{1,0:T(8,128)} fusion(bf16[768,2048]{1,0:T(8,128)(2,1)} %collective-permute-done, bf16[4,512,1536]{2,1,0:T(8,128)(2,1)S(1)} %bitcast.120, s32[]{:T(128)S(6)} %select_n.147, s32[]{:T(128)S(6)} %select_n.148), kind=kOutput, calls=%fused_computation.13 | convolution fusion | flops 1610612736 | bytes 8126472 | tf_op jit(solution)/shard_map/dot_general | solution.py:197
  319.0 5.8 %fusion.6 = f32[512,2048]{1,0:T(8,128)} fusion(bf16[768,2048]{1,0:T(8,128)(2,1)} %collective-permute-done.3, bf16[4,512,1536]{2,1,0:T(8,128)(2,1)S(1)} %bitcast.121, s32[]{:T(128)S(6)} %select_n.159, s32[]{:T(128)S(6)} %select_n.160), kind=kOutput, calls=%fused_computation.7 | convolution fusion | flops 1610612736 | bytes 8126472 | tf_op jit(solution)/shard_map/dot_general | solution.py:197
  324.8 5.7 %fusion.10 = f32[512,2048]{1,0:T(8,128)} fusion(bf16[768,2048]{1,0:T(8,128)(2,1)} %collective-permute-done.1, bf16[4,512,1536]{2,1,0:T(8,128)(2,1)S(1)} %bitcast.122, s32[]{:T(128)S(6)} %select_n.151, s32[]{:T(128)S(6)} %select_n.152), kind=kOutput, calls=%fused_computation.11 | convolution fusion | flops 1610612736 | bytes 8126472 | tf_op jit(solution)/shard_map/dot_general | solution.py:197
  330.5 4.7 fusion.23
  335.2 4.8 fusion.25
  340.0 17.7 %multiply_reduce_fusion = (f32[512]{0:T(512)S(1)}, f32[512]{0:T(512)S(1)}, f32[512,2048]{1,0:T(8,128)}) fusion(f32[512,2048]{1,0:T(8,128)S(1)} %copy-done.7, f32[512,2048]{1,0:T(8,128)} %fusion.23, f32[512,2048]{1,0:T(8,128)} %fusion.25, bf16[768,2048]{1,0:T(8,128)(2,1)} %collective-permute-done.5, bf16[4,512,1536]{2,1,0:T(8,128)(2,1)} %bitcast.117, ...), kind=kOutput, calls=%fused_computation | convolution fusion | flops 1624243200 | bytes 45887496 | tf_op jit(solution)/shard_map/dot_general | solution.py:197
  357.7 5.6 %all-reduce = (f32[512]{0:T(512)S(1)}, f32[512]{0:T(512)S(1)}) all-reduce(f32[512]{0:T(512)S(1)} %get-tuple-element.34, f32[512]{0:T(512)S(1)} %get-tuple-element.33), channel_id=1, replica_groups=mesh['ctx'=8,'head'=4] {'head'}, use_global_device_ids=true, to_apply=%region_4.5 | all-reduce | flops 1024 | bytes 8192 | tf_op jit(solution)/shard_map/psum | solution.py:279
  363.6 1.6 copy-done.4
  365.2 1.6 copy-done.9
  368.0 22.2 %shard_map.123 = (bf16[512,2048]{1,0:T(8,128)(2,1)}, f32[512,2048]{1,0:T(8,128)}, f32[512,2048]{1,0:T(8,128)}, f32[2,16,128,128]{3,2,1,0:T(8,128)S(1)}, bf16[16,128,128]{2,1,0:T(8,128)(2,1)}) custom-call(f32[16]{0:T(128)S(1)} %copy-done.16, f32[3,2]{1,0:T(4,128)S(1)} %pad_maximum_fusion.carries, bf16[512,2048]{1,0:T(8,128)(2,1)S(1)} %copy-done.9, ...), custom_call_target="tpu_custom_call" | custom-call | flops 3221225472 | bytes 25165824 | tf_op jit(solution)/shard_map/pallas_call | solution.py:166
  391.6 74.6 %all-gather.11.cloned.1.call-done = bf16[128,128,128]{2,1,0:T(8,128)(2,1)} async-done(((bf16[16,128,128]{2,1,0:T(8,128)(2,1)}), bf16[128,128,128]{2,1,0:T(8,128)(2,1)}) %all-gather.11.cloned.1.call-update) | async-done | bytes 4194320 | tf_op jit(solution)/shard_map/all_gather | solution.py:294
  466.2 1.6 copy-done.5
  467.8 2.2 copy-done.10
  470.0 1.6 copy-done.12
  471.6 13.4 %shard_map.124 = (bf16[512,2048]{1,0:T(8,128)(2,1)}, bf16[512,2048]{1,0:T(8,128)(2,1)}) custom-call(f32[16]{0:T(128)S(1)} %copy-done.16, f32[3,2]{1,0:T(4,128)S(1)} %pad_maximum_fusion.carries, f32[8,16]{1,0:T(8,128)S(1)} %get-tuple-element.53.coef_ref, bf16[8,16,128,128]{3,2,1,0:T(8,128)(2,1)S(1)} %bitcast.111, bf16[512,2048]{1,0:T(8,128)(2,1)S(1)} %copy-done.1, ...), custom_call_target="tpu_custom_call" | custom-call | flops 536870912 | bytes 20971520 | tf_op jit(solution)/shard_map/pallas_call | solution.py:166
  (89 shorter events, 18.5 us)
Async XLA Ops:
  7.2 214.2 %copy-start.20 = (s32[8]{0:T(128)S(1)}, s32[8]{0:T(128)}, u32[]{:S(2)}) copy-start(s32[8]{0:T(128)} %constant.203.clone) | copy-start | bytes 100
  7.2 221.2 %copy-start.18 = (s32[8]{0:T(128)S(1)}, s32[8]{0:T(128)}, u32[]{:S(2)}) copy-start(s32[8]{0:T(128)} %constant.202.clone) | copy-start | bytes 100
  7.2 227.8 %copy-start.16 = (f32[16]{0:T(128)S(1)}, f32[16]{0:T(128)}, u32[]{:S(2)}) copy-start(f32[16]{0:T(128)} %slopes.7) | copy-start | bytes 196
  7.2 229.7 %all-gather.9.cloned.1.call-start = ((), (), s32[]{:S(2)}) async-start(), calls=%async_computation.1 | async-start | bytes 4718592 | tf_op jit(solution)/shard_map/all_gather | solution.py:268
  14.4 1.6 copy-start
  16.0 1.6 copy-start.2
  17.6 0.7 copy-start.15
  18.3 218.6 %copy-start.1 = (bf16[512,2048]{1,0:T(8,128)(2,1)S(1)}, bf16[512,2048]{1,0:T(8,128)(2,1)}, u32[]{:S(2)}) copy-start(bf16[512,2048]{1,0:T(8,128)(2,1)} %k_ref.7) | copy-start | bytes 6291460
  27.6 267.9 %all-gather.7.cloned.1.call-start = ((), (), s32[]{:S(2)}) async-start(), calls=%async_computation | async-start | bytes 7864320 | tf_op jit(solution)/shard_map/all_gather | solution.py:269
  27.7 122.0 %collective-permute-start.1 = (bf16[768,2048]{1,0:T(8,128)(2,1)}, bf16[768,2048]{1,0:T(8,128)(2,1)}, u32[]{:S(2)}, u32[]{:S(2)}) collective-permute-start(bf16[768,2048]{1,0:T(8,128)(2,1)} %param.16), channel_id=1, source_target_pairs={{8,0},{16,8},{24,16},{28,24},{20,28},{12,20},{4,12},{0,4},{9,1},{1... | collective-permute-start | bytes 9437192 | tf_op jit(solution)/shard_map/ppermute | solution.py:203
  30.7 119.7 %collective-permute-start = (bf16[768,2048]{1,0:T(8,128)(2,1)}, bf16[768,2048]{1,0:T(8,128)(2,1)}, u32[]{:S(2)}, u32[]{:S(2)}) collective-permute-start(bf16[768,2048]{1,0:T(8,128)(2,1)} %param.16), channel_id=1, source_target_pairs={{0,8},{8,16},{16,24},{24,28},{28,20},{20,12},{12,4},{4,0},{1,9},{9... | collective-permute-start | bytes 9437192 | tf_op jit(solution)/shard_map/ppermute | solution.py:202
  30.8 435.4 %all-gather.11.cloned.1.call-start = ((), (), s32[]{:S(2)}) async-start(), calls=%async_computation.2 | async-start | bytes 4718592 | tf_op jit(solution)/shard_map/all_gather | solution.py:294
  149.7 69.6 %collective-permute-start.3 = (bf16[768,2048]{1,0:T(8,128)(2,1)}, bf16[768,2048]{1,0:T(8,128)(2,1)}, u32[]{:S(2)}, u32[]{:S(2)}) collective-permute-start(bf16[768,2048]{1,0:T(8,128)(2,1)} %collective-permute-done.1), channel_id=1, source_target_pairs={{8,0},{16,8},{24,16},{28,24},{20,28},{12,20},{4,12},{0,4},{9,1},{1... | collective-permute-start | bytes 9437192 | tf_op jit(solution)/shard_map/ppermute | solution.py:203
  150.4 69.5 %collective-permute-start.2 = (bf16[768,2048]{1,0:T(8,128)(2,1)}, bf16[768,2048]{1,0:T(8,128)(2,1)}, u32[]{:S(2)}, u32[]{:S(2)}) collective-permute-start(bf16[768,2048]{1,0:T(8,128)(2,1)} %collective-permute-done), channel_id=1, source_target_pairs={{0,8},{8,16},{16,24},{24,28},{28,20},{20,12},{12,4},{4,0},{1,9},{9... | collective-permute-start | bytes 9437192 | tf_op jit(solution)/shard_map/ppermute | solution.py:202
  219.3 68.7 %collective-permute-start.5 = (bf16[768,2048]{1,0:T(8,128)(2,1)}, bf16[768,2048]{1,0:T(8,128)(2,1)}, u32[]{:S(2)}, u32[]{:S(2)}) collective-permute-start(bf16[768,2048]{1,0:T(8,128)(2,1)} %collective-permute-done.3), channel_id=1, source_target_pairs={{8,0},{16,8},{24,16},{28,24},{20,28},{12,20},{4,12},{0,4},{9,1},{1... | collective-permute-start | bytes 9437192 | tf_op jit(solution)/shard_map/ppermute | solution.py:203
  219.9 71.1 %collective-permute-start.4 = (bf16[768,2048]{1,0:T(8,128)(2,1)}, bf16[768,2048]{1,0:T(8,128)(2,1)}, u32[]{:S(2)}, u32[]{:S(2)}) collective-permute-start(bf16[768,2048]{1,0:T(8,128)(2,1)} %collective-permute-done.2), channel_id=1, source_target_pairs={{0,8},{8,16},{16,24},{24,28},{28,20},{20,12},{12,4},{4,0},{1,9},{9... | collective-permute-start | bytes 9437192 | tf_op jit(solution)/shard_map/ppermute | solution.py:202
  236.9 1.6 copy-start.3
  238.5 1.6 copy-start.8
  253.6 2.1 copy-start.6
  255.6 1.0 copy-start.13
  290.7 39.7 %collective-permute-start.7 = (bf16[384,2048]{1,0:T(8,128)(2,1)}, bf16[384,2048]{1,0:T(8,128)(2,1)}, u32[]{:S(2)}, u32[]{:S(2)}) collective-permute-start(bf16[384,2048]{1,0:T(8,128)(2,1)} %slice.47), channel_id=1, source_target_pairs={{8,0},{16,8},{24,16},{28,24},{20,28},{12,20},{4,12},{0,4},{9,1},{1... | collective-permute-start | bytes 4718600 | tf_op jit(solution)/shard_map/ppermute | solution.py:209
  293.8 41.4 %collective-permute-start.6 = (bf16[384,2048]{1,0:T(8,128)(2,1)}, bf16[384,2048]{1,0:T(8,128)(2,1)}, u32[]{:S(2)}, u32[]{:S(2)}) collective-permute-start(bf16[384,2048]{1,0:T(8,128)(2,1)} %slice.46), channel_id=1, source_target_pairs={{0,8},{8,16},{16,24},{24,28},{28,20},{20,12},{12,4},{4,0},{1,9},{9... | collective-permute-start | bytes 4718600 | tf_op jit(solution)/shard_map/ppermute | solution.py:208
  295.5 6.2 %copy-start.17 = (bf16[2048,1536]{1,0:T(8,128)(2,1)S(1)}, bf16[2048,1536]{1,0:T(8,128)(2,1)}, u32[]{:S(2)}) copy-start(bf16[2048,1536]{1,0:T(8,128)(2,1)} %all-gather.7.cloned.1.call-done) | copy-start | bytes 18874372
  335.2 4.8 copy-start.7
  335.2 4.8 copy-start.19
  363.6 1.6 copy-start.4
  365.2 1.6 copy-start.9
  366.7 1.2 copy-start.14
  390.2 1.3 copy-start.11
  466.2 1.6 copy-start.5
  467.8 2.2 copy-start.10
  470.0 1.6 copy-start.12
Sparse Core Ops, SparseCore 0:
  27.8 121.2 all-gather.8
  150.7 48.8 all-gather.6
  391.7 74.4 all-gather.10

commit v2 on v1

--- a/solution.py
+++ b/solution.py
@@ -52,13 +52,6 @@
     return pl.ds(b * BLK, BLK)
 
 
-def weighted(coef_ref, gathered_ref, head):
-    total = jnp.zeros((DH, DH), jnp.float32)
-    for j in range(gathered_ref.shape[0]):
-        total += coef_ref[j, head] * gathered_ref[j, 0].astype(jnp.float32)
-    return total
-
-
 def next_state(state, k, v, table, slope, carry):
     faded = jnp.exp(-slope * (BLK - 1.0 - places())) * table[:, TAIL : TAIL + 1]
     update = dot((k.astype(jnp.float32) * faded).astype(jnp.bfloat16), v, 0, 0)
@@ -78,12 +71,11 @@
 
 
 def forward_kernel(
-    slopes, carries, coef_ref, gathered_ref, q_ref, k_ref, v_ref, table_ref, col_ref, row_ref,
+    slopes, carries, entering_ref, q_ref, k_ref, v_ref, table_ref, col_ref, row_ref,
     attended_ref, used_ref,
 ):
-    head = pl.program_id(0)
-    slope = slopes[head]
-    state = weighted(coef_ref, gathered_ref, head)
+    slope = slopes[pl.program_id(0)]
+    state = entering_ref[0].astype(jnp.float32)
     for b in range(blocks_of(q_ref)):
         q, k, v = q_ref[rows(b), :], k_ref[rows(b), :], v_ref[rows(b), :]
         table = table_ref[rows(b), :]
@@ -96,41 +88,49 @@
         state = next_state(state, k, v, table, slope, carries[0, b])
 
 
-def backward_kernel(
-    slopes, carries, q_ref, k_ref, v_ref, gained_ref, attended_ref, used_ref, table_ref, col_ref,
-    row_ref, dq_ref, dk_ref, dv_ref, local_ref, total_ref,
+def delta_kernel(
+    slopes, carries, q_ref, gained_ref, attended_ref, table_ref, delta_ref, local_ref, total_ref
 ):
     slope = slopes[pl.program_id(0)]
     state = jnp.zeros((DH, DH), jnp.float32)
     for b in reversed(range(blocks_of(q_ref))):
-        q, k, v = q_ref[rows(b), :], k_ref[rows(b), :], v_ref[rows(b), :]
         table = table_ref[rows(b), :]
         delta = (
             table[:, SCALE : SCALE + 1] * gained_ref[rows(b), :]
             - table[:, CROSS : CROSS + 1] * attended_ref[rows(b), :]
         ).astype(jnp.bfloat16)
+        delta_ref[rows(b), :] = delta
+        local_ref[b, 0] = state
+        leading = jnp.exp(-slope * places()) * table[:, LEAD : LEAD + 1]
+        faded = (q_ref[rows(b), :].astype(jnp.float32) * leading).astype(jnp.bfloat16)
+        state = (carries[1, b] * tile_exp(slope, BLK)) * state + dot(faded, delta, 0, 0)
+    total_ref[0] = state.astype(total_ref.dtype)
+
+
+def backward_kernel(
+    slopes, q_ref, k_ref, v_ref, delta_ref, used_ref, table_ref, col_ref, row_ref,
+    dq_ref, dk_ref, dv_ref,
+):
+    slope = slopes[pl.program_id(0)]
+    for b in range(blocks_of(q_ref)):
+        q, k, v = q_ref[rows(b), :], k_ref[rows(b), :], v_ref[rows(b), :]
+        delta = delta_ref[rows(b), :]
         decays = decays_of(col_ref[rows(b), :], row_ref[:, rows(b)], slope)
         fwd_weights = (dot(q, k, 1, 1) * decays).astype(jnp.bfloat16)
         back_weights = (dot(delta, v, 1, 1) * decays).astype(jnp.bfloat16)
-        entering = jnp.exp(-slope * (places() + 1.0)) * table[:, ENTER : ENTER + 1]
+        entering = jnp.exp(-slope * (places() + 1.0)) * table_ref[rows(b), ENTER : ENTER + 1]
         dq = dot(back_weights, k, 1, 0) + entering * dot(delta, used_ref[b, 0], 1, 1)
         dq_ref[rows(b), :] = dq.astype(dq_ref.dtype)
         dk_ref[rows(b), :] = dot(back_weights, q, 0, 0)
         dv_ref[rows(b), :] = dot(fwd_weights, delta, 0, 0)
-        local_ref[b, 0] = state
-        leading = jnp.exp(-slope * places()) * table[:, LEAD : LEAD + 1]
-        faded = (q.astype(jnp.float32) * leading).astype(jnp.bfloat16)
-        state = (carries[1, b] * tile_exp(slope, BLK)) * state + dot(faded, delta, 0, 0)
-    total_ref[0] = state.astype(total_ref.dtype)
 
 
 def finish_kernel(
-    slopes, carries, coef_ref, gathered_ref, k_ref, v_ref, local_ref, table_ref, dk_ref, dv_ref,
+    slopes, carries, entering_ref, k_ref, v_ref, local_ref, table_ref, dk_ref, dv_ref,
     dk_out, dv_out,
 ):
-    head = pl.program_id(0)
-    slope = slopes[head]
-    entering = weighted(coef_ref, gathered_ref, head)
+    slope = slopes[pl.program_id(0)]
+    entering = entering_ref[0].astype(jnp.float32)
     count = blocks_of(k_ref)
     for b in range(count):
         reach = carries[2, b] * tile_exp(slope, BLK * (count - 1 - b))
@@ -178,7 +178,7 @@
     return [*range(0, count, 2), *range(count - 1 - count % 2, 0, -2)]
 
 
-def ring_matmul(dy, weight, count):
+def ring_matmul(dy, weight, count, beside, forward):
     order = ring_order(count)
     table = jnp.asarray(order, jnp.int32)
     spot = [order.index(i) for i in range(count)]
@@ -196,20 +196,71 @@
         )[0]
         return jnp.dot(part, block, preferred_element_type=jnp.float32)
 
+    full = (count - 1) // 2
+    from_left = lax.ppermute(weight, "ctx", up)
+    from_right = lax.ppermute(weight, "ctx", down)
+    from_left, from_right, beside = lax.optimization_barrier((from_left, from_right, beside))
+    result = forward(*beside)
     total = term(weight, 0, 0)
-    from_left = from_right = weight
-    for step in range(1, (count - 1) // 2 + 1):
-        from_left = lax.ppermute(from_left, "ctx", up)
-        from_right = lax.ppermute(from_right, "ctx", down)
-        total = total + term(from_left, -step, 0)
-        total = total + term(from_right, step, 0)
-    if count % 2 == 0:
-        half = depth // 2
-        left = lax.ppermute(from_left[:half], "ctx", up)
-        right = lax.ppermute(from_right[half:], "ctx", down)
-        total = total + term(left, -(count // 2), 0)
-        total = total + term(right, count // 2, half)
-    return total
+    for step in range(2, full + 1):
+        left = lax.ppermute(from_left, "ctx", up)
+        right = lax.ppermute(from_right, "ctx", down)
+        total = total + term(from_left, 1 - step, 0)
+        total = total + term(from_right, step - 1, 0)
+        if step == full:
+            result, left, right, total = lax.optimization_barrier((result, left, right, total))
+        else:
+            left, right, total = lax.optimization_barrier((left, right, total))
+        from_left, from_right = left, right
+    half = depth // 2
+    left = lax.ppermute(from_left[:half], "ctx", up)
+    right = lax.ppermute(from_right[half:], "ctx", down)
+    total = total + term(from_left, -full, 0)
+    total = total + term(from_right, full, 0)
+    left, right, total = lax.optimization_barrier((left, right, total))
+    total = total + term(left, -(count // 2), 0)
+    total = total + term(right, count // 2, half)
+    return total, result
+
+
+def exchange(local, marks, slopes, tokens, reverse):
+    count = lax.axis_size("ctx")
+    half = local.shape[0] // 2
+    index = lambda i: count - 1 - i if reverse else i
+    me = index(lax.axis_index("ctx"))
+    marks = marks[::-1] if reverse else marks
+    high, low = me // 2, me % 2
+    swap = [(i, i ^ 1) for i in range(count)]
+    f32 = jnp.float32
+
+    def part(array, which):
+        return lax.dynamic_slice_in_dim(array, which * half, half)
+
+    def fade(rate, hops, same):
+        return jnp.where(same, jnp.exp(-rate * (hops * tokens)), 0.0)[:, None, None]
+
+    mine = part(local, low)
+    other = lax.ppermute(part(local, 1 - low), "ctx", swap)
+    rate = part(slopes, low)
+    first = jnp.where(low == 0, mine, other).astype(f32)
+    second = jnp.where(low == 0, other, mine).astype(f32)
+    pair = second + fade(rate, 1, marks[2 * high] == marks[2 * high + 1]) * first
+    pair = pair.astype(jnp.bfloat16)
+    last = marks[jnp.maximum(2 * high - 1, 0)]
+    into_first = jnp.zeros(pair.shape, f32)
+    for hop in range(1, count // 2):
+        moves = [(index(i), index(i + 2 * hop)) for i in range(count - 2 * hop)]
+        came = lax.ppermute(pair, "ctx", moves)
+        from_high = high - hop
+        same = (from_high >= 0) & (marks[jnp.maximum(2 * from_high + 1, 0)] == last)
+        into_first = into_first + fade(rate, 2 * (hop - 1), same) * came.astype(f32)
+    same = (high > 0) & (marks[2 * high] == last)
+    into_second = first + fade(rate, 1, same) * into_first
+    into_first, into_second = into_first.astype(jnp.bfloat16), into_second.astype(jnp.bfloat16)
+    keep = jnp.where(low == 0, into_first, into_second)
+    came = lax.ppermute(jnp.where(low == 0, into_second, into_first), "ctx", swap)
+    front = jnp.where(low == 0, keep, came)
+    return jnp.concatenate([front, jnp.where(low == 0, came, keep)])
 
 
 def per_device(queries, keys, values, out_grad, out_weight, norm_gain, slopes, resp_lengths):
@@ -245,13 +296,6 @@
     ends = segment_ids(resp_lengths, spans * tokens + (tokens - 1), RESP)
     starts = segment_ids(resp_lengths, spans * tokens, RESP)
 
-    def coefficients(hops, same):
-        faded = jnp.exp(-slopes[None, :] * (jnp.maximum(hops, 0) * tokens)[:, None].astype(jnp.float32))
-        return jnp.where(((hops >= 0) & same)[:, None], faded, 0.0)
-
-    fwd_coef = coefficients(me - 1 - spans, ends == before)
-    bwd_coef = coefficients(spans - me - 1, starts == beyond)
-
     f32, bf16 = jnp.float32, jnp.bfloat16
     sheet = lambda kind: jax.ShapeDtypeStruct((tokens, width), kind)
     states = jax.ShapeDtypeStruct((heads, DH, DH), bf16)
@@ -261,20 +305,23 @@
     unit = 2 * tokens * BLK * width
     size = 2 * tokens * width
 
-    local = call(
-        summary_kernel, heads, [smem(), smem(), col, col, table_spec], one_state(), states,
-        (slopes, carries, keys, values, table), unit // 2, 2 * size,
-    )
-    gathered = lax.all_gather(local, "ctx")
+    def forward(queries, keys, values):
+        local = call(
+            summary_kernel, heads, [smem(), smem(), col, col, table_spec], one_state(), states,
+            (slopes, carries, keys, values, table), unit // 2, 2 * size,
+        )
+        entering = exchange(local, ends, slopes, tokens, False)
+        return call(
+            forward_kernel, heads,
+            [smem(), smem(), one_state(), col, col, col, table_spec, *seg_specs],
+            (col, stack(blocks)), (sheet(f32), per_head(bf16)),
+            (slopes, carries, entering, queries, keys, values, table, seg_col, seg_row),
+            3 * unit, 6 * size,
+        )
+
     dy = lax.all_gather(out_grad, "head")
-    norm_grad = ring_matmul(dy, out_weight, count)
-
-    attended, used = call(
-        forward_kernel, heads,
-        [smem(), smem(), smem(), stack(count), col, col, col, table_spec, *seg_specs],
-        (col, stack(blocks)), (sheet(f32), per_head(bf16)),
-        (slopes, carries, fwd_coef, gathered, queries, keys, values, table, seg_col, seg_row),
-        3 * unit, 9 * size,
+    norm_grad, (attended, used) = ring_matmul(
+        dy, out_weight, count, (queries, keys, values), forward
     )
     square_total = lax.psum(jnp.sum(attended * attended, axis=1), "head")
     rescale = lax.rsqrt(square_total / (HEADS * DH) + EPSILON)
@@ -283,20 +330,24 @@
     cross_mean = cross_total / (HEADS * DH)
     back_table = jnp.stack(masks + [valid * rescale, valid * rescale**3 * cross_mean], axis=1)
 
-    dq, dk, dv, inner, total = call(
+    delta, inner, total = call(
+        delta_kernel, heads, [smem(), smem(), col, col, col, table_spec],
+        (col, stack(blocks), one_state()), (sheet(bf16), per_head(f32), states),
+        (slopes, carries, queries, gained, attended, back_table), unit // 2, 7 * size,
+    )
+    leaving = exchange(total, starts, slopes, tokens, True)
+    dq, dk, dv = call(
         backward_kernel, heads,
-        [smem(), smem(), col, col, col, col, col, stack(blocks), table_spec, *seg_specs],
-        (col, col, col, stack(blocks), one_state()),
-        (sheet(bf16), sheet(f32), sheet(f32), per_head(f32), states),
-        (slopes, carries, queries, keys, values, gained, attended, used, back_table, seg_col, seg_row),
-        6 * unit, 12 * size,
-    )
-    back_gathered = lax.all_gather(total, "ctx")
+        [smem(), col, col, col, col, stack(blocks), table_spec, *seg_specs],
+        (col, col, col), (sheet(bf16), sheet(f32), sheet(f32)),
+        (slopes, queries, keys, values, delta, used, table, seg_col, seg_row),
+        6 * unit, 10 * size,
+    )
     dk, dv = call(
         finish_kernel, heads,
-        [smem(), smem(), smem(), stack(count), col, col, stack(blocks), table_spec, col, col],
+        [smem(), smem(), one_state(), col, col, stack(blocks), table_spec, col, col],
         (col, col), (sheet(bf16), sheet(bf16)),
-        (slopes, carries, bwd_coef, back_gathered, keys, values, inner, table, dk, dv),
+        (slopes, carries, leaving, keys, values, inner, table, dk, dv),
         unit, 10 * size,
     )
     return dq, dk, dv

time: 493 us -> 434 us (0.88)
  waiting for transfers between devices: 293 us -> 209 us
  starting transfers between devices: 9.07 us -> 29.9 us
  matrix products: 62.2 us -> 42.2 us
  between operations: 26.3 us -> 39.4 us
    all_gather x2 -> x0, waiting for transfers between devices: 74.6 us -> none  [the longest x1 74.6 us: per_device(): back_gathered = lax.all_gather(total, 'ctx')]
    ppermute x6 -> x16, waiting for transfers between devices: 218 us -> 188 us  [the longest x6 90.8 us: exchange(): came = lax.ppermute(pair, 'ctx', moves)]
    dot_general x9, matrix products: 62.2 us -> 42.2 us  [term(): return jnp.dot(part, block, preferred_element_type=jnp.float32)]
    ppermute x1, waiting for transfers between devices: 0.01 us -> 15.5 us  [ring_matmul(): left = lax.ppermute(from_left[:half], 'ctx', up)]
    ppermute x6 -> x16, starting transfers between devices: 6.92 us -> 22 us  [the longest x6 13.5 us: exchange(): came = lax.ppermute(pair, 'ctx', moves)]
    ppermute x1, starting transfers between devices: 1.74 us -> 7.84 us  [ring_matmul(): left = lax.ppermute(from_left[:half], 'ctx', up)]
    select_n x1 -> x9, other arithmetic: 0.08 us -> 5.24 us  [the longest x2 1.96 us: exchange(): front = jnp.where(low == 0, keep, came)]
    pallas_call x4 -> x5, Pallas kernels: 58.4 us -> 62.9 us  [call(): pl.pallas_call(kernel, grid=(heads,), in_specs=in_specs, out_specs=out_sp...]
  transfers between devices with their start and end apart: 11 -> 19, of which waited for: 5 -> 13; matrix products, arithmetic and copies ran while one was open for 10% -> 12% of each run, Pallas kernels for 3% -> 9%
where the time goes in v2:
time: 434 us; the launch traced here: 432 us
  waiting for transfers between devices  209 us (48%)
  Pallas kernels  62.9 us (14%)
  matrix products  42.2 us (10%)
  between operations  39.4 us (9%)
  local copies, waits for them, and re-layouts  31.9 us (7%)
  starting transfers between devices  29.9 us (7%)
  other arithmetic  11 us (3%)
  blocking collectives  5.63 us (1%)
    ppermute x6, waiting for transfers between devices, exchange(): came = lax.ppermute(pair, 'ctx', moves)  90.8 us
    pallas_call x5, Pallas kernels, call(): pl.pallas_call(kernel, grid=(heads,), in_specs=in_specs, out_specs=out_sp...  62.9 us
    ppermute x1, waiting for transfers between devices, ring_matmul(): from_left = lax.ppermute(weight, 'ctx', up)  53.4 us
    dot_general x9, matrix products, term(): return jnp.dot(part, block, preferred_element_type=jnp.float32)  42.2 us
    ppermute x2, waiting for transfers between devices, ring_matmul(): left = lax.ppermute(from_left, 'ctx', up)  30.7 us
    unnamed x62, local copies, waits for them, and re-layouts  19.2 us
    ppermute x1, waiting for transfers between devices, ring_matmul(): left = lax.ppermute(from_left[:half], 'ctx', up)  15.5 us
    ppermute x6, starting transfers between devices, exchange(): came = lax.ppermute(pair, 'ctx', moves)  13.5 us
  transfers between devices with their start and end apart: 19, of which 13 were waited for; matrix products, arithmetic and copies ran while one was open for 12% of the time, Pallas kernels for 9%

profile of v2, /device:TPU:0, one launch (start us, length us, event | category | flops | bytes accessed | tf_op | source)
XLA Modules:
  0.0 431.8 jit_solution(17933419669306460853)
XLA Ops:
  7.9 3.1 collective-permute-start
  25.9 53.4 %collective-permute-done = bf16[768,2048]{1,0:T(8,128)(2,1)} collective-permute-done((bf16[768,2048]{1,0:T(8,128)(2,1)}, bf16[768,2048]{1,0:T(8,128)(2,1)}, u32[]{:S(2)}, u32[]{:S(2)}) %collective-permute-start) | collective-permute-done | bytes 3145760 | tf_op jit(solution)/shard_map/ppermute | solution.py:200
  100.1 7.6 %shard_map.121 = bf16[16,128,128]{2,1,0:T(8,128)(2,1)S(1)} custom-call(f32[16]{0:T(128)S(1)} %copy-done.14, f32[3,2]{1,0:T(4,128)S(1)} %pad_maximum_fusion.2.carries, bf16[512,2048]{1,0:T(8,128)(2,1)S(1)} %copy-done, bf16[512,2048]{1,0:T(8,128)(2,1)S(1)} %copy-done.2, f32[512,6]{1,0:T(8,128)S(1)} %copy.34.table_ref), custom_call_target="tpu_custom_call" | custom-call | flops 268435456 | bytes 4194304 | tf_op jit(solution)/shard_map/pallas_call | solution.py:166
  108.1 4.1 fusion.13
  112.3 3.1 fusion.15
  115.3 6.2 %add_add_fusion.2 = f32[512,2048]{1,0:T(8,128)} fusion(f32[512,2048]{1,0:T(8,128)S(1)} %fusion.15, f32[512,2048]{1,0:T(8,128)S(1)} %fusion.13, bf16[768,2048]{1,0:T(8,128)(2,1)} %collective-permute-done.1, bf16[4,512,1536]{2,1,0:T(8,128)(2,1)} %bitcast.127, s32[]{:T(128)S(6)} %select_n.328, s32[]{:T(128)S(6)} %select_n.329), kind=kOutput, calls=%fused_computation.5 | convolution fusion | flops 1612709888 | bytes 16515080 | tf_op jit(solution)/shard_map/dot_general | solution.py:197
  121.5 30.7 %collective-permute-done.7 = bf16[768,2048]{1,0:T(8,128)(2,1)} collective-permute-done((bf16[768,2048]{1,0:T(8,128)(2,1)}, bf16[768,2048]{1,0:T(8,128)(2,1)}, u32[]{:S(2)}, u32[]{:S(2)}) %collective-permute-start.7) | collective-permute-done | bytes 3145760 | tf_op jit(solution)/shard_map/ppermute | solution.py:206
  154.2 3.5 collective-permute-done.2
  159.2 7.1 %collective-permute-start.4 = (bf16[8,128,128]{2,1,0:T(8,128)(2,1)S(1)}, bf16[8,128,128]{2,1,0:T(8,128)(2,1)S(1)}, u32[]{:S(2)}, u32[]{:S(2)}) collective-permute-start(bf16[8,128,128]{2,1,0:T(8,128)(2,1)S(1)} %fusion.25), channel_id=1, source_target_pairs={{0,16},{4,20},{8,24},{12,28},{1,17},{5,21},{9,25},{13,29},{2,18},{... | collective-permute-start | bytes 786440 | tf_op jit(solution)/shard_map/ppermute | solution.py:253
  167.6 61.1 %collective-permute-done.3 = bf16[8,128,128]{2,1,0:T(8,128)(2,1)S(1)} collective-permute-done((bf16[8,128,128]{2,1,0:T(8,128)(2,1)S(1)}, bf16[8,128,128]{2,1,0:T(8,128)(2,1)S(1)}, u32[]{:S(2)}, u32[]{:S(2)}) %collective-permute-start.3) | collective-permute-done | bytes 262176 | tf_op jit(solution)/shard_map/ppermute | solution.py:253
  228.6 3.5 collective-permute-done.4
  232.1 2.8 collective-permute-done.5
  237.5 5.2 %collective-permute-done.6 = bf16[8,128,128]{2,1,0:T(8,128)(2,1)} collective-permute-done((bf16[8,128,128]{2,1,0:T(8,128)(2,1)}, bf16[8,128,128]{2,1,0:T(8,128)(2,1)}, u32[]{:S(2)}, u32[]{:S(2)}) %collective-permute-start.6) | collective-permute-done | bytes 262176 | tf_op jit(solution)/shard_map/ppermute | solution.py:261
  246.9 12.0 %shard_map.122 = (f32[512,2048]{1,0:T(8,128)S(1)}, bf16[2,16,128,128]{3,2,1,0:T(8,128)(2,1)S(1)}) custom-call(f32[16]{0:T(128)S(1)} %copy-done.15, f32[3,2]{1,0:T(4,128)S(1)} %pad_maximum_fusion.2.carries, bf16[16,128,128]{2,1,0:T(8,128)(2,1)S(1)} %pad_maximum_fusion.entering_ref, bf16[512,2048]{1,0:T(8,128)(2,1)S(1)} %copy-done.9, ...), custom_call_target="tpu_custom_call" | custom-call | flops 1610612736 | bytes 12582912 | tf_op jit(solution)/shard_map/pallas_call | solution.py:166
  259.0 5.9 %fusion.10 = f32[512,2048]{1,0:T(8,128)S(1)} fusion(bf16[768,2048]{1,0:T(8,128)(2,1)} %collective-permute-done.7, bf16[4,512,1536]{2,1,0:T(8,128)(2,1)} %bitcast.128, s32[]{:T(128)S(6)} %select_n.332, s32[]{:T(128)S(6)} %select_n.333), kind=kOutput, calls=%fused_computation.12 | convolution fusion | flops 1610612736 | bytes 8126472 | tf_op jit(solution)/shard_map/dot_general | solution.py:197
  264.9 6.2 %add_add_fusion.1 = f32[512,2048]{1,0:T(8,128)} fusion(f32[512,2048]{1,0:T(8,128)S(1)} %copy-done.21, f32[512,2048]{1,0:T(8,128)S(1)} %fusion.10, bf16[768,2048]{1,0:T(8,128)(2,1)} %collective-permute-done.8, bf16[4,512,1536]{2,1,0:T(8,128)(2,1)} %bitcast.129, s32[]{:T(128)S(6)} %select_n.336, s32[]{:T(128)S(6)} %select_n.337), kind=kOutput, calls=%fused_computation.4 | convolution fusion | flops 1612709888 | bytes 16515080 | tf_op jit(solution)/shard_map/dot_general | solution.py:197
  271.1 2.7 slice.44
  273.8 7.8 %collective-permute-start.11 = (bf16[384,2048]{1,0:T(8,128)(2,1)}, bf16[384,2048]{1,0:T(8,128)(2,1)}, u32[]{:S(2)}, u32[]{:S(2)}) collective-permute-start(bf16[384,2048]{1,0:T(8,128)(2,1)} %slice.44), channel_id=1, source_target_pairs={{0,8},{8,16},{16,24},{24,28},{28,20},{20,12},{12,4},{4,0},{1,9},{9... | collective-permute-start | bytes 4718600 | tf_op jit(solution)/shard_map/ppermute | solution.py:216
  281.7 2.7 slice.45
  287.0 4.1 fusion.4
  291.2 4.1 add_add_fusion
  295.4 15.5 %collective-permute-done.11 = bf16[384,2048]{1,0:T(8,128)(2,1)} collective-permute-done((bf16[384,2048]{1,0:T(8,128)(2,1)}, bf16[384,2048]{1,0:T(8,128)(2,1)}, u32[]{:S(2)}, u32[]{:S(2)}) %collective-permute-start.11) | collective-permute-done | bytes 1572896 | tf_op jit(solution)/shard_map/ppermute | solution.py:216
  310.9 4.9 %collective-permute-done.12 = bf16[384,2048]{1,0:T(8,128)(2,1)} collective-permute-done((bf16[384,2048]{1,0:T(8,128)(2,1)}, bf16[384,2048]{1,0:T(8,128)(2,1)}, u32[]{:S(2)}, u32[]{:S(2)}) %collective-permute-start.12) | collective-permute-done | bytes 1572896 | tf_op jit(solution)/shard_map/ppermute | solution.py:217
  315.8 2.9 fusion.34
  318.7 5.6 %multiply_reduce_fusion = (f32[512]{0:T(512)S(1)}, f32[512]{0:T(512)S(1)}, f32[512,2048]{1,0:T(8,128)}) fusion(f32[512,2048]{1,0:T(8,128)S(1)} %copy-done.7, bf16[384,2048]{1,0:T(8,128)(2,1)} %collective-permute-done.12, bf16[4,512,1536]{2,1,0:T(8,128)(2,1)} %bitcast.133, s32[]{:T(128)S(6)} %select_n.352, s32[]{:T(128)S(6)} %select_n.353, ...), kind=kOutput, calls=%fused_computation | convolution fusion | flops 812645376 | bytes 18755592 | tf_op jit(solution)/shard_map/dot_general | solution.py:197
  324.3 5.6 %all-reduce = (f32[512]{0:T(512)S(1)}, f32[512]{0:T(512)S(1)}) all-reduce(f32[512]{0:T(512)S(1)} %get-tuple-element.68, f32[512]{0:T(512)S(1)} %get-tuple-element.67), channel_id=1, replica_groups=mesh['ctx'=8,'head'=4] {'head'}, use_global_device_ids=true, to_apply=%region_4.5 | all-reduce | flops 1024 | bytes 8192 | tf_op jit(solution)/shard_map/psum | solution.py:326
  333.9 13.6 %shard_map.123 = (bf16[512,2048]{1,0:T(8,128)(2,1)S(1)}, f32[2,16,128,128]{3,2,1,0:T(8,128)S(1)}, bf16[16,128,128]{2,1,0:T(8,128)(2,1)S(1)}) custom-call(f32[16]{0:T(128)S(1)} %copy-done.15, f32[3,2]{1,0:T(4,128)S(1)} %pad_maximum_fusion.2.carries, bf16[512,2048]{1,0:T(8,128)(2,1)S(1)} %copy-done.10, f32[512,2048]{1,0:T(8,128)S(1)} %copy-done.8, ...), custom_call_target="tpu_custom_call" | custom-call | flops 268435456 | bytes 14680064 | tf_op jit(solution)/shard_map/pallas_call | solution.py:166
  356.5 2.7 collective-permute-done.13
  363.2 6.0 %collective-permute-done.14 = bf16[8,128,128]{2,1,0:T(8,128)(2,1)S(1)} collective-permute-done((bf16[8,128,128]{2,1,0:T(8,128)(2,1)S(1)}, bf16[8,128,128]{2,1,0:T(8,128)(2,1)S(1)}, u32[]{:S(2)}, u32[]{:S(2)}) %collective-permute-start.14) | collective-permute-done | bytes 262176 | tf_op jit(solution)/shard_map/ppermute | solution.py:253
  369.2 17.4 %collective-permute-done.15 = bf16[8,128,128]{2,1,0:T(8,128)(2,1)S(1)} collective-permute-done((bf16[8,128,128]{2,1,0:T(8,128)(2,1)S(1)}, bf16[8,128,128]{2,1,0:T(8,128)(2,1)S(1)}, u32[]{:S(2)}, u32[]{:S(2)}) %collective-permute-start.15) | collective-permute-done | bytes 262176 | tf_op jit(solution)/shard_map/ppermute | solution.py:253
  393.6 17.5 %shard_map.124 = (bf16[512,2048]{1,0:T(8,128)(2,1)}, f32[512,2048]{1,0:T(8,128)S(1)}, f32[512,2048]{1,0:T(8,128)}) custom-call(f32[16]{0:T(128)S(1)} %copy-done.15, bf16[512,2048]{1,0:T(8,128)(2,1)S(1)} %copy-done.11, bf16[512,2048]{1,0:T(8,128)(2,1)S(1)} %copy-done.1, bf16[512,2048]{1,0:T(8,128)(2,1)S(1)} %copy-done.4, bf16[512,2048]{1,0:T(8,128)(2,1)S(1)} %copy-done.17, ...), custom_call_target="tpu_custom_call" | custom-call | flops 3221225472 | bytes 20971520 | tf_op jit(solution)/shard_map/pallas_call | solution.py:166
  412.7 12.2 %shard_map.125 = (bf16[512,2048]{1,0:T(8,128)(2,1)}, bf16[512,2048]{1,0:T(8,128)(2,1)}) custom-call(f32[16]{0:T(128)S(1)} %copy-done.15, f32[3,2]{1,0:T(4,128)S(1)} %pad_maximum_fusion.2.carries, bf16[16,128,128]{2,1,0:T(8,128)(2,1)S(1)} %pad_maximum_fusion.1.entering_ref, bf16[512,2048]{1,0:T(8,128)(2,1)S(1)} %copy-done.1, bf16[512,2048]{1,0:T(8,128)(2,1)S(1)} %copy-done.5, ...), custom_call_target="tpu_custom_call" | custom-call | flops 536870912 | bytes 20971520 | tf_op jit(solution)/shard_map/pallas_call | solution.py:166
  (131 shorter events, 51.6 us)
Async XLA Ops:
  7.2 100.9 %all-gather.3.cloned.1.call-start = ((), (), s32[]{:S(2)}) async-start(), calls=%async_computation | async-start | bytes 7864320 | tf_op jit(solution)/shard_map/all_gather | solution.py:322
  7.9 71.4 %collective-permute-start = (bf16[768,2048]{1,0:T(8,128)(2,1)}, bf16[768,2048]{1,0:T(8,128)(2,1)}, u32[]{:S(2)}, u32[]{:S(2)}) collective-permute-start(bf16[768,2048]{1,0:T(8,128)(2,1)} %param.16), channel_id=1, source_target_pairs={{0,8},{8,16},{16,24},{24,28},{28,20},{20,12},{12,4},{4,0},{1,9},{9... | collective-permute-start | bytes 9437192 | tf_op jit(solution)/shard_map/ppermute | solution.py:200
  11.0 69.9 %collective-permute-start.1 = (bf16[768,2048]{1,0:T(8,128)(2,1)}, bf16[768,2048]{1,0:T(8,128)(2,1)}, u32[]{:S(2)}, u32[]{:S(2)}) collective-permute-start(bf16[768,2048]{1,0:T(8,128)(2,1)} %param.16), channel_id=1, source_target_pairs={{8,0},{16,8},{24,16},{28,24},{20,28},{12,20},{4,12},{0,4},{9,1},{1... | collective-permute-start | bytes 9437192 | tf_op jit(solution)/shard_map/ppermute | solution.py:201
  80.9 71.4 %collective-permute-start.7 = (bf16[768,2048]{1,0:T(8,128)(2,1)}, bf16[768,2048]{1,0:T(8,128)(2,1)}, u32[]{:S(2)}, u32[]{:S(2)}) collective-permute-start(bf16[768,2048]{1,0:T(8,128)(2,1)} %collective-permute-done), channel_id=1, source_target_pairs={{0,8},{8,16},{16,24},{24,28},{28,20},{20,12},{12,4},{4,0},{1,9},{9... | collective-permute-start | bytes 9437192 | tf_op jit(solution)/shard_map/ppermute | solution.py:206
  82.4 69.8 %collective-permute-start.8 = (bf16[768,2048]{1,0:T(8,128)(2,1)}, bf16[768,2048]{1,0:T(8,128)(2,1)}, u32[]{:S(2)}, u32[]{:S(2)}) collective-permute-start(bf16[768,2048]{1,0:T(8,128)(2,1)} %collective-permute-done.1), channel_id=1, source_target_pairs={{8,0},{16,8},{24,16},{28,24},{20,28},{12,20},{4,12},{0,4},{9,1},{1... | collective-permute-start | bytes 9437192 | tf_op jit(solution)/shard_map/ppermute | solution.py:207
  107.7 50.0 %collective-permute-start.2 = (bf16[8,128,128]{2,1,0:T(8,128)(2,1)S(1)}, bf16[8,128,128]{2,1,0:T(8,128)(2,1)S(1)}, u32[]{:S(2)}, u32[]{:S(2)}) collective-permute-start(bf16[8,128,128]{2,1,0:T(8,128)(2,1)S(1)} %constant_dynamic-slice_fusion.1), channel_id=1, source_target_pairs={{0,4},{4,0},{8,12},{12,8},{16,20},{20,16},{24,28},{28,24},{1,5},{5... | collective-permute-start | bytes 786440 | tf_op jit(solution)/shard_map/ppermute | solution.py:243
  108.1 4.1 copy-start.26
  121.5 123.8 %copy-start.1 = (bf16[512,2048]{1,0:T(8,128)(2,1)S(1)}, bf16[512,2048]{1,0:T(8,128)(2,1)}, u32[]{:S(2)}) copy-start(bf16[512,2048]{1,0:T(8,128)(2,1)} %k_ref.5) | copy-start | bytes 6291460
  121.5 123.8 %copy-start.15 = (f32[16]{0:T(128)S(1)}, f32[16]{0:T(128)}, u32[]{:S(2)}) copy-start(f32[16]{0:T(128)} %slopes.9) | copy-start | bytes 196
  152.2 118.9 %collective-permute-start.10 = (bf16[768,2048]{1,0:T(8,128)(2,1)}, bf16[768,2048]{1,0:T(8,128)(2,1)}, u32[]{:S(2)}, u32[]{:S(2)}) collective-permute-start(bf16[768,2048]{1,0:T(8,128)(2,1)} %collective-permute-done.8), channel_id=1, source_target_pairs={{8,0},{16,8},{24,16},{28,24},{20,28},{12,20},{4,12},{0,4},{9,1},{1... | collective-permute-start | bytes 9437192 | tf_op jit(solution)/shard_map/ppermute | solution.py:207
  154.2 116.9 %collective-permute-start.9 = (bf16[768,2048]{1,0:T(8,128)(2,1)}, bf16[768,2048]{1,0:T(8,128)(2,1)}, u32[]{:S(2)}, u32[]{:S(2)}) collective-permute-start(bf16[768,2048]{1,0:T(8,128)(2,1)} %collective-permute-done.7), channel_id=1, source_target_pairs={{0,8},{8,16},{16,24},{24,28},{28,20},{20,12},{12,4},{4,0},{1,9},{9... | collective-permute-start | bytes 9437192 | tf_op jit(solution)/shard_map/ppermute | solution.py:206
  157.9 70.8 %collective-permute-start.3 = (bf16[8,128,128]{2,1,0:T(8,128)(2,1)S(1)}, bf16[8,128,128]{2,1,0:T(8,128)(2,1)S(1)}, u32[]{:S(2)}, u32[]{:S(2)}) collective-permute-start(bf16[8,128,128]{2,1,0:T(8,128)(2,1)S(1)} %fusion.25), channel_id=1, source_target_pairs={{0,8},{4,12},{8,16},{12,20},{16,24},{20,28},{1,9},{5,13},{9,17},{1... | collective-permute-start | bytes 786440 | tf_op jit(solution)/shard_map/ppermute | solution.py:253
  159.2 73.0 %collective-permute-start.4 = (bf16[8,128,128]{2,1,0:T(8,128)(2,1)S(1)}, bf16[8,128,128]{2,1,0:T(8,128)(2,1)S(1)}, u32[]{:S(2)}, u32[]{:S(2)}) collective-permute-start(bf16[8,128,128]{2,1,0:T(8,128)(2,1)S(1)} %fusion.25), channel_id=1, source_target_pairs={{0,16},{4,20},{8,24},{12,28},{1,17},{5,21},{9,25},{13,29},{2,18},{... | collective-permute-start | bytes 786440 | tf_op jit(solution)/shard_map/ppermute | solution.py:253
  166.2 68.7 %collective-permute-start.5 = (bf16[8,128,128]{2,1,0:T(8,128)(2,1)S(1)}, bf16[8,128,128]{2,1,0:T(8,128)(2,1)S(1)}, u32[]{:S(2)}, u32[]{:S(2)}) collective-permute-start(bf16[8,128,128]{2,1,0:T(8,128)(2,1)S(1)} %fusion.25), channel_id=1, source_target_pairs={{0,24},{4,28},{1,25},{5,29},{2,26},{6,30},{3,27},{7,31}} | collective-permute-start | bytes 786440 | tf_op jit(solution)/shard_map/ppermute | solution.py:253
  228.6 8.7 %copy-start.22 = (bf16[8,128,128]{2,1,0:T(8,128)(2,1)}, bf16[8,128,128]{2,1,0:T(8,128)(2,1)S(1)}, u32[]{:S(2)}) copy-start(bf16[8,128,128]{2,1,0:T(8,128)(2,1)S(1)} %collective-permute-done.3) | copy-start | bytes 786436
  232.1 2.8 copy-start.23
  236.0 6.7 %collective-permute-start.6 = (bf16[8,128,128]{2,1,0:T(8,128)(2,1)}, bf16[8,128,128]{2,1,0:T(8,128)(2,1)}, u32[]{:S(2)}, u32[]{:S(2)}) collective-permute-start(bf16[8,128,128]{2,1,0:T(8,128)(2,1)} %broadcast_select_fusion.7), channel_id=1, source_target_pairs={{0,4},{4,0},{8,12},{12,8},{16,20},{20,16},{24,28},{28,24},{1,5},{5... | collective-permute-start | bytes 786440 | tf_op jit(solution)/shard_map/ppermute | solution.py:261
  237.5 7.8 %copy-start.3 = (bf16[512,2048]{1,0:T(8,128)(2,1)S(1)}, bf16[512,2048]{1,0:T(8,128)(2,1)}, u32[]{:S(2)}) copy-start(bf16[512,2048]{1,0:T(8,128)(2,1)} %v_ref.5) | copy-start | bytes 6291460
  258.9 5.9 %copy-start.6 = (f32[512,2048]{1,0:T(8,128)}, f32[512,2048]{1,0:T(8,128)S(1)}, u32[]{:S(2)}) copy-start(f32[512,2048]{1,0:T(8,128)S(1)} %get-tuple-element.57.attended_ref) | copy-start | bytes 12582916
  259.0 5.9 %copy-start.18 = (bf16[2,16,128,128]{3,2,1,0:T(8,128)(2,1)}, bf16[2,16,128,128]{3,2,1,0:T(8,128)(2,1)S(1)}, u32[]{:S(2)}) copy-start(bf16[2,16,128,128]{3,2,1,0:T(8,128)(2,1)S(1)} %get-tuple-element.59.used_ref) | copy-start | bytes 3145732
  259.0 5.9 %copy-start.21 = (f32[512,2048]{1,0:T(8,128)S(1)}, f32[512,2048]{1,0:T(8,128)}, u32[]{:S(2)}) copy-start(f32[512,2048]{1,0:T(8,128)} %add_add_fusion.2) | copy-start | bytes 12582916
  273.8 37.1 %collective-permute-start.11 = (bf16[384,2048]{1,0:T(8,128)(2,1)}, bf16[384,2048]{1,0:T(8,128)(2,1)}, u32[]{:S(2)}, u32[]{:S(2)}) collective-permute-start(bf16[384,2048]{1,0:T(8,128)(2,1)} %slice.44), channel_id=1, source_target_pairs={{0,8},{8,16},{16,24},{24,28},{28,20},{20,12},{12,4},{4,0},{1,9},{9... | collective-permute-start | bytes 4718600 | tf_op jit(solution)/shard_map/ppermute | solution.py:216
  284.4 31.4 %collective-permute-start.12 = (bf16[384,2048]{1,0:T(8,128)(2,1)}, bf16[384,2048]{1,0:T(8,128)(2,1)}, u32[]{:S(2)}, u32[]{:S(2)}) collective-permute-start(bf16[384,2048]{1,0:T(8,128)(2,1)} %slice.45), channel_id=1, source_target_pairs={{8,0},{16,8},{24,16},{28,24},{20,28},{12,20},{4,12},{0,4},{9,1},{1... | collective-permute-start | bytes 4718600 | tf_op jit(solution)/shard_map/ppermute | solution.py:217
  287.0 4.2 copy-start.20
  295.3 23.4 %copy-start.7 = (f32[512,2048]{1,0:T(8,128)S(1)}, f32[512,2048]{1,0:T(8,128)}, u32[]{:S(2)}) copy-start(f32[512,2048]{1,0:T(8,128)} %copy-done.6) | copy-start | bytes 12582916
  295.4 23.4 %copy-start.25 = (f32[2048]{0:T(1024)S(1)}, f32[2048]{0:T(1024)}, u32[]{:S(2)}) copy-start(f32[2048]{0:T(1024)} %param.17) | copy-start | bytes 24580
  350.9 8.3 %collective-permute-start.13 = (bf16[8,128,128]{2,1,0:T(8,128)(2,1)}, bf16[8,128,128]{2,1,0:T(8,128)(2,1)S(1)}, u32[]{:S(2)}, u32[]{:S(2)}) collective-permute-start(bf16[8,128,128]{2,1,0:T(8,128)(2,1)} %constant_dynamic-slice_fusion), channel_id=1, source_target_pairs={{0,4},{4,0},{8,12},{12,8},{16,20},{20,16},{24,28},{28,24},{1,5},{5... | collective-permute-start | bytes 786440 | tf_op jit(solution)/shard_map/ppermute | solution.py:243
  359.3 9.9 %collective-permute-start.14 = (bf16[8,128,128]{2,1,0:T(8,128)(2,1)S(1)}, bf16[8,128,128]{2,1,0:T(8,128)(2,1)S(1)}, u32[]{:S(2)}, u32[]{:S(2)}) collective-permute-start(bf16[8,128,128]{2,1,0:T(8,128)(2,1)S(1)} %fusion.28), channel_id=1, source_target_pairs={{28,20},{24,16},{20,12},{16,8},{12,4},{8,0},{29,21},{25,17},{21,13... | collective-permute-start | bytes 786440 | tf_op jit(solution)/shard_map/ppermute | solution.py:253
  360.6 26.0 %collective-permute-start.15 = (bf16[8,128,128]{2,1,0:T(8,128)(2,1)S(1)}, bf16[8,128,128]{2,1,0:T(8,128)(2,1)S(1)}, u32[]{:S(2)}, u32[]{:S(2)}) collective-permute-start(bf16[8,128,128]{2,1,0:T(8,128)(2,1)S(1)} %fusion.28), channel_id=1, source_target_pairs={{28,12},{24,8},{20,4},{16,0},{29,13},{25,9},{21,5},{17,1},{30,14},... | collective-permute-start | bytes 786440 | tf_op jit(solution)/shard_map/ppermute | solution.py:253
  361.9 24.7 %collective-permute-start.16 = (bf16[8,128,128]{2,1,0:T(8,128)(2,1)S(1)}, bf16[8,128,128]{2,1,0:T(8,128)(2,1)S(1)}, u32[]{:S(2)}, u32[]{:S(2)}) collective-permute-start(bf16[8,128,128]{2,1,0:T(8,128)(2,1)S(1)} %fusion.28), channel_id=1, source_target_pairs={{28,4},{24,0},{29,5},{25,1},{30,6},{26,2},{31,7},{27,3}} | collective-permute-start | bytes 786440 | tf_op jit(solution)/shard_map/ppermute | solution.py:253
  387.0 24.2 %collective-permute-start.17 = (bf16[8,128,128]{2,1,0:T(8,128)(2,1)S(1)}, bf16[8,128,128]{2,1,0:T(8,128)(2,1)S(1)}, u32[]{:S(2)}, u32[]{:S(2)}) collective-permute-start(bf16[8,128,128]{2,1,0:T(8,128)(2,1)S(1)} %broadcast_select_fusion.2), channel_id=1, source_target_pairs={{0,4},{4,0},{8,12},{12,8},{16,20},{20,16},{24,28},{28,24},{1,5},{5... | collective-permute-start | bytes 786440 | tf_op jit(solution)/shard_map/ppermute | solution.py:261
  393.6 18.1 %copy-start.13 = (f32[2,16,128,128]{3,2,1,0:T(8,128)S(1)}, f32[2,16,128,128]{3,2,1,0:T(8,128)}, u32[]{:S(2)}) copy-start(f32[2,16,128,128]{3,2,1,0:T(8,128)} %copy-done.12) | copy-start | bytes 6291460
  (14 other events, 20.5 us)
Sparse Core Ops, SparseCore 0:
  9.6 49.0 all-gather.2

commit v3 on v2

--- a/solution.py
+++ b/solution.py
@@ -10,7 +10,7 @@
 BLK = 256
 RESP = 8
 EPSILON = 1e-06
-VMEM_BYTES = 40 * 1024 * 1024
+PER = 2
 
 ENTER, EXIT, TAIL, LEAD, SCALE, CROSS = range(6)
 
@@ -60,8 +60,8 @@
     return (carry * tile_exp(slope, BLK)) * state + update
 
 
-def summary_kernel(slopes, carries, k_ref, v_ref, table_ref, out_ref):
-    slope = slopes[pl.program_id(0)]
+def summary_kernel(head, slopes, carries, k_ref, v_ref, table_ref, out_ref):
+    slope = slopes[head]
     state = None
     for b in range(blocks_of(k_ref)):
         state = next_state(
@@ -71,10 +71,10 @@
 
 
 def forward_kernel(
-    slopes, carries, entering_ref, q_ref, k_ref, v_ref, table_ref, col_ref, row_ref,
+    head, slopes, carries, entering_ref, q_ref, k_ref, v_ref, table_ref, col_ref, row_ref,
     attended_ref, used_ref,
 ):
-    slope = slopes[pl.program_id(0)]
+    slope = slopes[head]
     state = entering_ref[0].astype(jnp.float32)
     for b in range(blocks_of(q_ref)):
         q, k, v = q_ref[rows(b), :], k_ref[rows(b), :], v_ref[rows(b), :]
@@ -89,9 +89,9 @@
 
 
 def delta_kernel(
-    slopes, carries, q_ref, gained_ref, attended_ref, table_ref, delta_ref, local_ref, total_ref
+    head, slopes, carries, q_ref, gained_ref, attended_ref, table_ref, delta_ref, local_ref, total_ref
 ):
-    slope = slopes[pl.program_id(0)]
+    slope = slopes[head]
     state = jnp.zeros((DH, DH), jnp.float32)
     for b in reversed(range(blocks_of(q_ref))):
         table = table_ref[rows(b), :]
@@ -108,10 +108,10 @@
 
 
 def backward_kernel(
-    slopes, q_ref, k_ref, v_ref, delta_ref, used_ref, table_ref, col_ref, row_ref,
+    head, slopes, q_ref, k_ref, v_ref, delta_ref, used_ref, table_ref, col_ref, row_ref,
     dq_ref, dk_ref, dv_ref,
 ):
-    slope = slopes[pl.program_id(0)]
+    slope = slopes[head]
     for b in range(blocks_of(q_ref)):
         q, k, v = q_ref[rows(b), :], k_ref[rows(b), :], v_ref[rows(b), :]
         delta = delta_ref[rows(b), :]
@@ -126,10 +126,10 @@
 
 
 def finish_kernel(
-    slopes, carries, entering_ref, k_ref, v_ref, local_ref, table_ref, dk_ref, dv_ref,
+    head, slopes, carries, entering_ref, k_ref, v_ref, local_ref, table_ref, dk_ref, dv_ref,
     dk_out, dv_out,
 ):
-    slope = slopes[pl.program_id(0)]
+    slope = slopes[head]
     entering = entering_ref[0].astype(jnp.float32)
     count = blocks_of(k_ref)
     for b in range(count):
@@ -143,33 +143,49 @@
 
 
 def smem():
-    return pl.BlockSpec(memory_space=pltpu.SMEM)
+    return "smem", pl.BlockSpec(memory_space=pltpu.SMEM)
 
 
 def columns(tokens):
-    return pl.BlockSpec((tokens, DH), lambda h: (0, h))
+    return "columns", pl.BlockSpec((tokens, PER * DH), lambda h: (0, h))
 
 
 def whole(shape):
-    return pl.BlockSpec(shape, lambda h: (0,) * len(shape))
+    return "whole", pl.BlockSpec(shape, lambda h: (0,) * len(shape))
 
 
 def stack(count):
-    return pl.BlockSpec((count, 1, DH, DH), lambda h: (0, h, 0, 0))
+    return "stack", pl.BlockSpec((count, PER, DH, DH), lambda h: (0, h, 0, 0))
 
 
 def one_state():
-    return pl.BlockSpec((1, DH, DH), lambda h: (h, 0, 0))
+    return "state", pl.BlockSpec((PER, DH, DH), lambda h: (h, 0, 0))
+
+
+def view(kind, ref, i):
+    if kind == "columns":
+        return ref.at[:, pl.ds(i * DH, DH)]
+    if kind == "stack":
+        return ref.at[:, pl.ds(i, 1)]
+    if kind == "state":
+        return ref.at[pl.ds(i, 1)]
+    return ref
 
 
 def call(kernel, heads, in_specs, out_specs, out_shape, operands, flops, moved):
+    kinds = [kind for kind, _ in (*in_specs, *out_specs)]
+
+    def step(*refs):
+        for i in range(PER):
+            head = pl.program_id(0) * PER + i
+            kernel(head, *[view(kind, ref, i) for kind, ref in zip(kinds, refs)])
+
     return pl.pallas_call(
-        kernel,
-        grid=(heads,),
-        in_specs=in_specs,
-        out_specs=out_specs,
+        step,
+        grid=(heads // PER,),
+        in_specs=[spec for _, spec in in_specs],
+        out_specs=[spec for _, spec in out_specs],
         out_shape=out_shape,
-        compiler_params=pltpu.CompilerParams(vmem_limit_bytes=VMEM_BYTES),
         cost_estimate=pl.CostEstimate(flops=flops, bytes_accessed=moved, transcendentals=0),
     )(*operands)
 
@@ -178,7 +194,7 @@
     return [*range(0, count, 2), *range(count - 1 - count % 2, 0, -2)]
 
 
-def ring_matmul(dy, weight, count, beside, forward):
+def ring_matmul(dy, weight, count, stages):
     order = ring_order(count)
     table = jnp.asarray(order, jnp.int32)
     spot = [order.index(i) for i in range(count)]
@@ -197,27 +213,22 @@
         return jnp.dot(part, block, preferred_element_type=jnp.float32)
 
     full = (count - 1) // 2
-    from_left = lax.ppermute(weight, "ctx", up)
-    from_right = lax.ppermute(weight, "ctx", down)
-    from_left, from_right, beside = lax.optimization_barrier((from_left, from_right, beside))
-    result = forward(*beside)
+    half = depth // 2
+    result = next(stages)
+    left = lax.ppermute(weight, "ctx", up)
+    right = lax.ppermute(weight, "ctx", down)
+    left, right, result = lax.optimization_barrier((left, right, result))
     total = term(weight, 0, 0)
-    for step in range(2, full + 1):
-        left = lax.ppermute(from_left, "ctx", up)
-        right = lax.ppermute(from_right, "ctx", down)
-        total = total + term(from_left, 1 - step, 0)
-        total = total + term(from_right, step - 1, 0)
-        if step == full:
-            result, left, right, total = lax.optimization_barrier((result, left, right, total))
-        else:
-            left, right, total = lax.optimization_barrier((left, right, total))
-        from_left, from_right = left, right
-    half = depth // 2
-    left = lax.ppermute(from_left[:half], "ctx", up)
-    right = lax.ppermute(from_right[half:], "ctx", down)
-    total = total + term(from_left, -full, 0)
-    total = total + term(from_right, full, 0)
-    left, right, total = lax.optimization_barrier((left, right, total))
+    for step in range(1, full + 1):
+        last = step == full
+        result = stages.send(result)
+        new_left = lax.ppermute(left[:half] if last else left, "ctx", up)
+        new_right = lax.ppermute(right[half:] if last else right, "ctx", down)
+        total = total + term(left, -step, 0)
+        total = total + term(right, step, 0)
+        left, right, total, result = lax.optimization_barrier(
+            (new_left, new_right, total, result)
+        )
     total = total + term(left, -(count // 2), 0)
     total = total + term(right, count // 2, half)
     return total, result
@@ -240,7 +251,7 @@
         return jnp.where(same, jnp.exp(-rate * (hops * tokens)), 0.0)[:, None, None]
 
     mine = part(local, low)
-    other = lax.ppermute(part(local, 1 - low), "ctx", swap)
+    other = yield lax.ppermute(part(local, 1 - low), "ctx", swap)
     rate = part(slopes, low)
     first = jnp.where(low == 0, mine, other).astype(f32)
     second = jnp.where(low == 0, other, mine).astype(f32)
@@ -248,9 +259,10 @@
     pair = pair.astype(jnp.bfloat16)
     last = marks[jnp.maximum(2 * high - 1, 0)]
     into_first = jnp.zeros(pair.shape, f32)
-    for hop in range(1, count // 2):
-        moves = [(index(i), index(i + 2 * hop)) for i in range(count - 2 * hop)]
-        came = lax.ppermute(pair, "ctx", moves)
+    hops = range(1, count // 2)
+    moves = [[(index(i), index(i + 2 * hop)) for i in range(count - 2 * hop)] for hop in hops]
+    arrived = yield [lax.ppermute(pair, "ctx", move) for move in moves]
+    for hop, came in zip(hops, arrived):
         from_high = high - hop
         same = (from_high >= 0) & (marks[jnp.maximum(2 * from_high + 1, 0)] == last)
         into_first = into_first + fade(rate, 2 * (hop - 1), same) * came.astype(f32)
@@ -258,9 +270,16 @@
     into_second = first + fade(rate, 1, same) * into_first
     into_first, into_second = into_first.astype(jnp.bfloat16), into_second.astype(jnp.bfloat16)
     keep = jnp.where(low == 0, into_first, into_second)
-    came = lax.ppermute(jnp.where(low == 0, into_second, into_first), "ctx", swap)
+    came = yield lax.ppermute(jnp.where(low == 0, into_second, into_first), "ctx", swap)
     front = jnp.where(low == 0, keep, came)
     return jnp.concatenate([front, jnp.where(low == 0, came, keep)])
+
+
+def finish_exchange(steps, arrived):
+    try:
+        steps.send(arrived)
+    except StopIteration as end:
+        return end.value
 
 
 def per_device(queries, keys, values, out_grad, out_weight, norm_gain, slopes, resp_lengths):
@@ -305,24 +324,24 @@
     unit = 2 * tokens * BLK * width
     size = 2 * tokens * width
 
-    def forward(queries, keys, values):
-        local = call(
-            summary_kernel, heads, [smem(), smem(), col, col, table_spec], one_state(), states,
+    def forward():
+        (local,) = call(
+            summary_kernel, heads, [smem(), smem(), col, col, table_spec], [one_state()], [states],
             (slopes, carries, keys, values, table), unit // 2, 2 * size,
         )
-        entering = exchange(local, ends, slopes, tokens, False)
-        return call(
+        entering = yield from exchange(local, ends, slopes, tokens, False)
+        result = call(
             forward_kernel, heads,
             [smem(), smem(), one_state(), col, col, col, table_spec, *seg_specs],
-            (col, stack(blocks)), (sheet(f32), per_head(bf16)),
+            [col, stack(blocks)], [sheet(f32), per_head(bf16)],
             (slopes, carries, entering, queries, keys, values, table, seg_col, seg_row),
             3 * unit, 6 * size,
         )
+        while True:
+            result = yield result
 
     dy = lax.all_gather(out_grad, "head")
-    norm_grad, (attended, used) = ring_matmul(
-        dy, out_weight, count, (queries, keys, values), forward
-    )
+    norm_grad, (attended, used) = ring_matmul(dy, out_weight, count, forward())
     square_total = lax.psum(jnp.sum(attended * attended, axis=1), "head")
     rescale = lax.rsqrt(square_total / (HEADS * DH) + EPSILON)
     gained = norm_gain[None, :] * norm_grad
@@ -332,21 +351,24 @@
 
     delta, inner, total = call(
         delta_kernel, heads, [smem(), smem(), col, col, col, table_spec],
-        (col, stack(blocks), one_state()), (sheet(bf16), per_head(f32), states),
+        [col, stack(blocks), one_state()], [sheet(bf16), per_head(f32), states],
         (slopes, carries, queries, gained, attended, back_table), unit // 2, 7 * size,
     )
-    leaving = exchange(total, starts, slopes, tokens, True)
+    steps = exchange(total, starts, slopes, tokens, True)
+    arrived = steps.send(next(steps))
     dq, dk, dv = call(
         backward_kernel, heads,
         [smem(), col, col, col, col, stack(blocks), table_spec, *seg_specs],
-        (col, col, col), (sheet(bf16), sheet(f32), sheet(f32)),
+        [col, col, col], [sheet(bf16), sheet(f32), sheet(f32)],
         (slopes, queries, keys, values, delta, used, table, seg_col, seg_row),
         6 * unit, 10 * size,
     )
+    arrived, dq, dk, dv = lax.optimization_barrier((arrived, dq, dk, dv))
+    leaving = finish_exchange(steps, steps.send(arrived))
     dk, dv = call(
         finish_kernel, heads,
         [smem(), smem(), one_state(), col, col, stack(blocks), table_spec, col, col],
-        (col, col), (sheet(bf16), sheet(bf16)),
+        [col, col], [sheet(bf16), sheet(bf16)],
         (slopes, carries, leaving, keys, values, inner, table, dk, dv),
         unit, 10 * size,
     )

time: 434 us -> 385 us (0.89)
  waiting for transfers between devices: 209 us -> 180 us
  local copies, waits for them, and re-layouts: 31.9 us -> 16.5 us
  Pallas kernels: 62.9 us -> 55.2 us
  starting transfers between devices: 29.9 us -> 34.9 us
  matrix products: 42.2 us -> 37.4 us
    ppermute x16, waiting for transfers between devices: 203 us -> 123 us  [the longest x2 57.6 us: exchange(): other = (yield lax.ppermute(part(local, 1 - low), 'ctx', swap))]
    ppermute x2, waiting for transfers between devices: 5.17 us -> 56.1 us  [exchange(): lax.ppermute(jnp.where(low == 0, into_second, into_first), 'ctx', swap)]
    unnamed x62 -> x38, local copies, waits for them, and re-layouts: 19.2 us -> 3.63 us
    pallas_call x5, Pallas kernels: 62.9 us -> 55.2 us  [call(): pl.pallas_call(step, grid=(heads // PER,), in_specs=[spec for _, spec in...]
    dot_general x9, matrix products: 42.2 us -> 37.4 us  [term(): return jnp.dot(part, block, preferred_element_type=jnp.float32)]
  transfers between devices with their start and end apart: 19 -> 19, of which waited for: 13 -> 10; matrix products, arithmetic and copies ran while one was open for 12% -> 12% of each run, Pallas kernels for 9% -> 9%
where the time goes in v3:
time: 385 us; the launch traced here: 383 us
  waiting for transfers between devices  180 us (47%)
  Pallas kernels  55.2 us (14%)
  between operations  38.9 us (10%)
  matrix products  37.4 us (10%)
  starting transfers between devices  34.9 us (9%)
  local copies, waits for them, and re-layouts  16.5 us (4%)
  other arithmetic  14.6 us (4%)
  blocking collectives  5.63 us (1%)
    ppermute x2, waiting for transfers between devices, exchange(): other = (yield lax.ppermute(part(local, 1 - low), 'ctx', swap))  57.6 us
    ppermute x2, waiting for transfers between devices, exchange(): lax.ppermute(jnp.where(low == 0, into_second, into_first), 'ctx', swap)  56.1 us
    pallas_call x5, Pallas kernels, call(): pl.pallas_call(step, grid=(heads // PER,), in_specs=[spec for _, spec in...  55.2 us
    ppermute x6, waiting for transfers between devices, exchange(): arrived = (yield [lax.ppermute(pair, 'ctx', move) for move in moves])  50.8 us
    dot_general x9, matrix products, term(): return jnp.dot(part, block, preferred_element_type=jnp.float32)  37.4 us
    ppermute x6, starting transfers between devices, exchange(): arrived = (yield [lax.ppermute(pair, 'ctx', move) for move in moves])  16.1 us
    ppermute x3, waiting for transfers between devices, ring_matmul(): new_left = lax.ppermute(left[:half] if last else left, 'ctx', up)  11 us
  transfers between devices with their start and end apart: 19, of which 10 were waited for; matrix products, arithmetic and copies ran while one was open for 12% of the time, Pallas kernels for 9%

profile of v3, /device:TPU:0, one launch (start us, length us, event | category | flops | bytes accessed | tf_op | source)
XLA Modules:
  0.0 382.6 jit_solution(2360611976692183352)
XLA Ops:
  7.9 3.1 collective-permute-start
  13.4 2.0 fusion.50
  19.5 7.8 %shard_map.121 = bf16[16,128,128]{2,1,0:T(8,128)(2,1)} custom-call(f32[16]{0:T(128)} %refs_0_.9, f32[3,2]{1,0:T(4,128)} %pad_maximum_fusion.2.refs_1_, bf16[512,2048]{1,0:T(8,128)(2,1)} %refs_3_.7, bf16[512,2048]{1,0:T(8,128)(2,1)} %refs_4_.3, f32[512,6]{1,0:T(8,128)} %copy.34.refs_4_.refs_6_), custom_call_target="tpu_custom_call" | custom-call | flops 268435456 | bytes 4194304 | tf_op jit(solution)/shard_map/pallas_call | solution.py:183
  30.3 54.5 %collective-permute-done.2 = bf16[8,128,128]{2,1,0:T(8,128)(2,1)S(1)} collective-permute-done((bf16[8,128,128]{2,1,0:T(8,128)(2,1)S(1)}, bf16[8,128,128]{2,1,0:T(8,128)(2,1)S(1)}, u32[]{:S(2)}, u32[]{:S(2)}) %collective-permute-start.2) | collective-permute-done | bytes 262176 | tf_op jit(solution)/shard_map/ppermute | solution.py:254
  109.0 2.6 collective-permute-start.5
  111.6 7.6 %collective-permute-start.6 = (bf16[8,128,128]{2,1,0:T(8,128)(2,1)}, bf16[8,128,128]{2,1,0:T(8,128)(2,1)}, u32[]{:S(2)}, u32[]{:S(2)}) collective-permute-start(bf16[8,128,128]{2,1,0:T(8,128)(2,1)} %fusion.25), channel_id=1, source_target_pairs={{0,16},{4,20},{8,24},{12,28},{1,17},{5,21},{9,25},{13,29},{2,18},{... | collective-permute-start | bytes 786440 | tf_op jit(solution)/shard_map/ppermute | solution.py:264
  121.2 4.1 %fusion.13 = f32[512,2048]{1,0:T(8,128)S(1)} fusion(bf16[768,2048]{1,0:T(8,128)(2,1)} %collective-permute-done, bf16[4,512,1536]{2,1,0:T(8,128)(2,1)} %bitcast.122, s32[]{:T(128)S(6)} %select_n.304, s32[]{:T(128)S(6)} %select_n.305), kind=kOutput, calls=%fused_computation.15 | convolution fusion | flops 1610612736 | bytes 8126472 | tf_op jit(solution)/shard_map/dot_general | solution.py:213
  125.4 3.2 fusion.15
  128.6 5.1 %add_add_fusion.2 = f32[512,2048]{1,0:T(8,128)} fusion(f32[512,2048]{1,0:T(8,128)S(1)} %fusion.15, f32[512,2048]{1,0:T(8,128)S(1)} %fusion.13, bf16[768,2048]{1,0:T(8,128)(2,1)S(1)} %copy-done.7, bf16[4,512,1536]{2,1,0:T(8,128)(2,1)} %bitcast.124, s32[]{:T(128)S(6)} %select_n.308, s32[]{:T(128)S(6)} %select_n.309), kind=kOutput, calls=%fused_computation.5 | convolution fusion | flops 1612709888 | bytes 16515080 | tf_op jit(solution)/shard_map/dot_general | solution.py:213
  133.7 27.3 %collective-permute-done.5 = bf16[8,128,128]{2,1,0:T(8,128)(2,1)} collective-permute-done((bf16[8,128,128]{2,1,0:T(8,128)(2,1)}, bf16[8,128,128]{2,1,0:T(8,128)(2,1)}, u32[]{:S(2)}, u32[]{:S(2)}) %collective-permute-start.5) | collective-permute-done | bytes 262176 | tf_op jit(solution)/shard_map/ppermute | solution.py:264
  161.0 5.7 %collective-permute-done.6 = bf16[8,128,128]{2,1,0:T(8,128)(2,1)} collective-permute-done((bf16[8,128,128]{2,1,0:T(8,128)(2,1)}, bf16[8,128,128]{2,1,0:T(8,128)(2,1)}, u32[]{:S(2)}, u32[]{:S(2)}) %collective-permute-start.6) | collective-permute-done | bytes 262176 | tf_op jit(solution)/shard_map/ppermute | solution.py:264
  166.6 4.2 %collective-permute-done.7 = bf16[8,128,128]{2,1,0:T(8,128)(2,1)} collective-permute-done((bf16[8,128,128]{2,1,0:T(8,128)(2,1)}, bf16[8,128,128]{2,1,0:T(8,128)(2,1)}, u32[]{:S(2)}, u32[]{:S(2)}) %collective-permute-start.7) | collective-permute-done | bytes 262176 | tf_op jit(solution)/shard_map/ppermute | solution.py:264
  172.4 6.1 %collective-permute-start.8 = (bf16[768,2048]{1,0:T(8,128)(2,1)}, bf16[768,2048]{1,0:T(8,128)(2,1)}, u32[]{:S(2)}, u32[]{:S(2)}) collective-permute-start(bf16[768,2048]{1,0:T(8,128)(2,1)} %collective-permute-done.3), channel_id=1, source_target_pairs={{0,8},{8,16},{16,24},{24,28},{28,20},{20,12},{12,4},{4,0},{1,9},{9... | collective-permute-start | bytes 9437192 | tf_op jit(solution)/shard_map/ppermute | solution.py:225
  184.9 2.8 collective-permute-start.10
  187.8 4.0 %fusion.10 = f32[512,2048]{1,0:T(8,128)S(1)} fusion(bf16[768,2048]{1,0:T(8,128)(2,1)} %collective-permute-done.3, bf16[4,512,1536]{2,1,0:T(8,128)(2,1)} %bitcast.125, s32[]{:T(128)S(6)} %select_n.322, s32[]{:T(128)S(6)} %select_n.323), kind=kOutput, calls=%fused_computation.12 | convolution fusion | flops 1610612736 | bytes 8126472 | tf_op jit(solution)/shard_map/dot_general | solution.py:213
  191.8 5.2 %add_add_fusion.1 = f32[512,2048]{1,0:T(8,128)} fusion(f32[512,2048]{1,0:T(8,128)S(1)} %copy-done, f32[512,2048]{1,0:T(8,128)S(1)} %fusion.10, bf16[768,2048]{1,0:T(8,128)(2,1)S(1)} %copy-done.5, bf16[4,512,1536]{2,1,0:T(8,128)(2,1)} %bitcast.126, s32[]{:T(128)S(6)} %select_n.326, s32[]{:T(128)S(6)} %select_n.327), kind=kOutput, calls=%fused_computation.4 | convolution fusion | flops 1612709888 | bytes 16515080 | tf_op jit(solution)/shard_map/dot_general | solution.py:213
  197.0 50.3 %collective-permute-done.10 = bf16[8,128,128]{2,1,0:T(8,128)(2,1)S(1)} collective-permute-done((bf16[8,128,128]{2,1,0:T(8,128)(2,1)S(1)}, bf16[8,128,128]{2,1,0:T(8,128)(2,1)S(1)}, u32[]{:S(2)}, u32[]{:S(2)}) %collective-permute-start.10) | collective-permute-done | bytes 262176 | tf_op jit(solution)/shard_map/ppermute | solution.py:273
  248.9 2.7 slice.44
  255.7 11.3 %shard_map.122 = (f32[512,2048]{1,0:T(8,128)}, bf16[2,16,128,128]{3,2,1,0:T(8,128)(2,1)}) custom-call(f32[16]{0:T(128)} %refs_0_.9, f32[3,2]{1,0:T(4,128)} %pad_maximum_fusion.2.refs_1_, bf16[16,128,128]{2,1,0:T(8,128)(2,1)} %pad_maximum_fusion.refs_2_, bf16[512,2048]{1,0:T(8,128)(2,1)} %refs_1_.1, bf16[512,2048]{1,0:T(8,128)(2,1)} %refs_3_.7, ...), custom_call_target="tpu_custom_call" | custom-call | flops 1610612736 | bytes 12582912 | tf_op jit(solution)/shard_map/pallas_call | solution.py:183
  267.1 4.1 %fusion.4 = f32[512,2048]{1,0:T(8,128)S(1)} fusion(bf16[768,2048]{1,0:T(8,128)(2,1)} %collective-permute-done.8, bf16[4,512,1536]{2,1,0:T(8,128)(2,1)} %bitcast.127, s32[]{:T(128)S(6)} %select_n.339, s32[]{:T(128)S(6)} %select_n.340), kind=kOutput, calls=%fused_computation.8 | convolution fusion | flops 1610612736 | bytes 8126472 | tf_op jit(solution)/shard_map/dot_general | solution.py:213
  271.2 3.2 add_add_fusion
  274.4 11.0 %collective-permute-done.11 = bf16[384,2048]{1,0:T(8,128)(2,1)} collective-permute-done((bf16[384,2048]{1,0:T(8,128)(2,1)}, bf16[384,2048]{1,0:T(8,128)(2,1)}, u32[]{:S(2)}, u32[]{:S(2)}) %collective-permute-start.11) | collective-permute-done | bytes 1572896 | tf_op jit(solution)/shard_map/ppermute | solution.py:225
  285.4 3.3 collective-permute-done.12
  288.7 2.9 fusion.34
  291.6 5.6 %multiply_reduce_fusion = (f32[512]{0:T(512)S(1)}, f32[512]{0:T(512)S(1)}, f32[512,2048]{1,0:T(8,128)}) fusion(f32[512,2048]{1,0:T(8,128)S(1)} %copy-done.2, bf16[384,2048]{1,0:T(8,128)(2,1)} %collective-permute-done.12, bf16[4,512,1536]{2,1,0:T(8,128)(2,1)} %bitcast.130, s32[]{:T(128)S(6)} %select_n.354, s32[]{:T(128)S(6)} %select_n.355, ...), kind=kOutput, calls=%fused_computation | convolution fusion | flops 812645376 | bytes 18755592 | tf_op jit(solution)/shard_map/dot_general | solution.py:213
  297.2 5.6 %all-reduce = (f32[512]{0:T(512)S(1)}, f32[512]{0:T(512)S(1)}) all-reduce(f32[512]{0:T(512)S(1)} %get-tuple-element.84, f32[512]{0:T(512)S(1)} %get-tuple-element.83), channel_id=1, replica_groups=mesh['ctx'=8,'head'=4] {'head'}, use_global_device_ids=true, to_apply=%region_4.5 | all-reduce | flops 1024 | bytes 8192 | tf_op jit(solution)/shard_map/psum | solution.py:345
  303.7 11.2 %shard_map.123 = (bf16[512,2048]{1,0:T(8,128)(2,1)}, f32[2,16,128,128]{3,2,1,0:T(8,128)}, bf16[16,128,128]{2,1,0:T(8,128)(2,1)}) custom-call(f32[16]{0:T(128)} %refs_0_.9, f32[3,2]{1,0:T(4,128)} %pad_maximum_fusion.2.refs_1_, bf16[512,2048]{1,0:T(8,128)(2,1)} %refs_1_.1, f32[512,2048]{1,0:T(8,128)} %get-tuple-element.142.refs_3_, ...), custom_call_target="tpu_custom_call" | custom-call | flops 268435456 | bytes 14680064 | tf_op jit(solution)/shard_map/pallas_call | solution.py:183
  321.0 3.1 collective-permute-done.13
  329.0 14.9 %shard_map.124 = (bf16[512,2048]{1,0:T(8,128)(2,1)}, f32[512,2048]{1,0:T(8,128)}, f32[512,2048]{1,0:T(8,128)}) custom-call(f32[16]{0:T(128)} %refs_0_.9, bf16[512,2048]{1,0:T(8,128)(2,1)} %refs_1_.1, bf16[512,2048]{1,0:T(8,128)(2,1)} %refs_3_.7, bf16[512,2048]{1,0:T(8,128)(2,1)} %refs_4_.3, bf16[512,2048]{1,0:T(8,128)(2,1)} %get-tuple-element.69.refs_4_, ...), custom_call_target="tpu_custom_call" | custom-call | flops 3221225472 | bytes 20971520 | tf_op jit(solution)/shard_map/pallas_call | solution.py:183
  343.9 13.7 %collective-permute-done.15 = bf16[8,128,128]{2,1,0:T(8,128)(2,1)S(1)} collective-permute-done((bf16[8,128,128]{2,1,0:T(8,128)(2,1)S(1)}, bf16[8,128,128]{2,1,0:T(8,128)(2,1)S(1)}, u32[]{:S(2)}, u32[]{:S(2)}) %collective-permute-start.15) | collective-permute-done | bytes 262176 | tf_op jit(solution)/shard_map/ppermute | solution.py:264
  358.7 5.8 %collective-permute-done.17 = bf16[8,128,128]{2,1,0:T(8,128)(2,1)S(1)} collective-permute-done((bf16[8,128,128]{2,1,0:T(8,128)(2,1)S(1)}, bf16[8,128,128]{2,1,0:T(8,128)(2,1)S(1)}, u32[]{:S(2)}, u32[]{:S(2)}) %collective-permute-start.17) | collective-permute-done | bytes 262176 | tf_op jit(solution)/shard_map/ppermute | solution.py:273
  365.8 10.0 %shard_map.125 = (bf16[512,2048]{1,0:T(8,128)(2,1)}, bf16[512,2048]{1,0:T(8,128)(2,1)}) custom-call(f32[16]{0:T(128)} %refs_0_.9, f32[3,2]{1,0:T(4,128)} %pad_maximum_fusion.2.refs_1_, bf16[16,128,128]{2,1,0:T(8,128)(2,1)} %pad_maximum_fusion.1.refs_2_, bf16[512,2048]{1,0:T(8,128)(2,1)} %refs_3_.7, bf16[512,2048]{1,0:T(8,128)(2,1)} %refs_4_.3, ...), custom_call_target="tpu_custom_call" | custom-call | flops 536870912 | bytes 20971520 | tf_op jit(solution)/shard_map/pallas_call | solution.py:183
  (107 shorter events, 39.7 us)
Async XLA Ops:
  7.2 81.4 %copy-start.14 = (s32[8]{0:T(128)S(1)}, s32[8]{0:T(128)}, u32[]{:S(2)}) copy-start(s32[8]{0:T(128)} %constant.260.clone) | copy-start | bytes 100
  7.2 87.9 %copy-start.9 = (s32[8]{0:T(128)S(1)}, s32[8]{0:T(128)}, u32[]{:S(2)}) copy-start(s32[8]{0:T(128)} %constant.259.clone) | copy-start | bytes 100
  7.2 99.9 %copy-start.10 = (f32[16]{0:T(128)S(1)}, f32[16]{0:T(128)}, u32[]{:S(2)}) copy-start(f32[16]{0:T(128)} %refs_0_.9) | copy-start | bytes 196
  7.2 114.0 %all-gather.3.cloned.1.call-start = ((), (), s32[]{:S(2)}) async-start(), calls=%async_computation | async-start | bytes 7864320 | tf_op jit(solution)/shard_map/all_gather | solution.py:343
  7.9 76.9 %collective-permute-start = (bf16[768,2048]{1,0:T(8,128)(2,1)}, bf16[768,2048]{1,0:T(8,128)(2,1)}, u32[]{:S(2)}, u32[]{:S(2)}) collective-permute-start(bf16[768,2048]{1,0:T(8,128)(2,1)} %param.16), channel_id=1, source_target_pairs={{0,8},{8,16},{16,24},{24,28},{28,20},{20,12},{12,4},{4,0},{1,9},{9... | collective-permute-start | bytes 9437192 | tf_op jit(solution)/shard_map/ppermute | solution.py:218
  11.0 73.9 %collective-permute-start.1 = (bf16[768,2048]{1,0:T(8,128)(2,1)}, bf16[768,2048]{1,0:T(8,128)(2,1)S(1)}, u32[]{:S(2)}, u32[]{:S(2)}) collective-permute-start(bf16[768,2048]{1,0:T(8,128)(2,1)} %param.16), channel_id=1, source_target_pairs={{8,0},{16,8},{24,16},{28,24},{20,28},{12,20},{4,12},{0,4},{9,1},{1... | collective-permute-start | bytes 9437192 | tf_op jit(solution)/shard_map/ppermute | solution.py:219
  12.0 170.5 %copy-start.11 = (s32[512]{0:T(512)}, s32[512]{0:T(512)S(1)}, u32[]{:S(2)}) copy-start(s32[512]{0:T(512)S(1)} %slice.37) | copy-start | bytes 6148
  28.3 56.6 %collective-permute-start.2 = (bf16[8,128,128]{2,1,0:T(8,128)(2,1)S(1)}, bf16[8,128,128]{2,1,0:T(8,128)(2,1)S(1)}, u32[]{:S(2)}, u32[]{:S(2)}) collective-permute-start(bf16[8,128,128]{2,1,0:T(8,128)(2,1)S(1)} %constant_dynamic-slice_fusion.1), channel_id=1, source_target_pairs={{0,4},{4,0},{8,12},{12,8},{16,20},{20,16},{24,28},{28,24},{1,5},{5... | collective-permute-start | bytes 786440 | tf_op jit(solution)/shard_map/ppermute | solution.py:254
  86.5 84.3 %collective-permute-start.3 = (bf16[768,2048]{1,0:T(8,128)(2,1)}, bf16[768,2048]{1,0:T(8,128)(2,1)}, u32[]{:S(2)}, u32[]{:S(2)}) collective-permute-start(bf16[768,2048]{1,0:T(8,128)(2,1)} %collective-permute-done), channel_id=1, source_target_pairs={{0,8},{8,16},{16,24},{24,28},{28,20},{20,12},{12,4},{4,0},{1,9},{9... | collective-permute-start | bytes 9437192 | tf_op jit(solution)/shard_map/ppermute | solution.py:225
  86.5 84.3 %collective-permute-start.4 = (bf16[768,2048]{1,0:T(8,128)(2,1)}, bf16[768,2048]{1,0:T(8,128)(2,1)S(1)}, u32[]{:S(2)}, u32[]{:S(2)}) collective-permute-start(bf16[768,2048]{1,0:T(8,128)(2,1)} %copy-done.6), channel_id=1, source_target_pairs={{8,0},{16,8},{24,16},{28,24},{20,28},{12,20},{4,12},{0,4},{9,1},{1... | collective-permute-start | bytes 9437192 | tf_op jit(solution)/shard_map/ppermute | solution.py:226
  109.0 51.9 %collective-permute-start.5 = (bf16[8,128,128]{2,1,0:T(8,128)(2,1)}, bf16[8,128,128]{2,1,0:T(8,128)(2,1)}, u32[]{:S(2)}, u32[]{:S(2)}) collective-permute-start(bf16[8,128,128]{2,1,0:T(8,128)(2,1)} %fusion.25), channel_id=1, source_target_pairs={{0,8},{4,12},{8,16},{12,20},{16,24},{20,28},{1,9},{5,13},{9,17},{1... | collective-permute-start | bytes 786440 | tf_op jit(solution)/shard_map/ppermute | solution.py:264
  111.6 55.0 %collective-permute-start.6 = (bf16[8,128,128]{2,1,0:T(8,128)(2,1)}, bf16[8,128,128]{2,1,0:T(8,128)(2,1)}, u32[]{:S(2)}, u32[]{:S(2)}) collective-permute-start(bf16[8,128,128]{2,1,0:T(8,128)(2,1)} %fusion.25), channel_id=1, source_target_pairs={{0,16},{4,20},{8,24},{12,28},{1,17},{5,21},{9,25},{13,29},{2,18},{... | collective-permute-start | bytes 786440 | tf_op jit(solution)/shard_map/ppermute | solution.py:264
  119.2 51.6 %collective-permute-start.7 = (bf16[8,128,128]{2,1,0:T(8,128)(2,1)}, bf16[8,128,128]{2,1,0:T(8,128)(2,1)}, u32[]{:S(2)}, u32[]{:S(2)}) collective-permute-start(bf16[8,128,128]{2,1,0:T(8,128)(2,1)} %fusion.25), channel_id=1, source_target_pairs={{0,24},{4,28},{1,25},{5,29},{2,26},{6,30},{3,27},{7,31}} | collective-permute-start | bytes 786440 | tf_op jit(solution)/shard_map/ppermute | solution.py:264
  121.2 4.1 %copy-start.13 = (bf16[768,2048]{1,0:T(8,128)(2,1)S(1)}, bf16[768,2048]{1,0:T(8,128)(2,1)}, u32[]{:S(2)}) copy-start(bf16[768,2048]{1,0:T(8,128)(2,1)} %param.16) | copy-start | bytes 9437188
  125.4 3.2 copy-start.7
  172.4 74.9 %collective-permute-start.8 = (bf16[768,2048]{1,0:T(8,128)(2,1)}, bf16[768,2048]{1,0:T(8,128)(2,1)}, u32[]{:S(2)}, u32[]{:S(2)}) collective-permute-start(bf16[768,2048]{1,0:T(8,128)(2,1)} %collective-permute-done.3), channel_id=1, source_target_pairs={{0,8},{8,16},{16,24},{24,28},{28,20},{20,12},{12,4},{4,0},{1,9},{9... | collective-permute-start | bytes 9437192 | tf_op jit(solution)/shard_map/ppermute | solution.py:225
  178.6 68.8 %collective-permute-start.9 = (bf16[768,2048]{1,0:T(8,128)(2,1)}, bf16[768,2048]{1,0:T(8,128)(2,1)S(1)}, u32[]{:S(2)}, u32[]{:S(2)}) collective-permute-start(bf16[768,2048]{1,0:T(8,128)(2,1)} %copy-done.4), channel_id=1, source_target_pairs={{8,0},{16,8},{24,16},{28,24},{20,28},{12,20},{4,12},{0,4},{9,1},{1... | collective-permute-start | bytes 9437192 | tf_op jit(solution)/shard_map/ppermute | solution.py:226
  184.9 6.8 %copy-start = (f32[512,2048]{1,0:T(8,128)S(1)}, f32[512,2048]{1,0:T(8,128)}, u32[]{:S(2)}) copy-start(f32[512,2048]{1,0:T(8,128)} %add_add_fusion.2) | copy-start | bytes 12582916
  184.9 6.8 %copy-start.5 = (bf16[768,2048]{1,0:T(8,128)(2,1)S(1)}, bf16[768,2048]{1,0:T(8,128)(2,1)}, u32[]{:S(2)}) copy-start(bf16[768,2048]{1,0:T(8,128)(2,1)} %copy-done.4) | copy-start | bytes 9437188
  184.9 62.4 %collective-permute-start.10 = (bf16[8,128,128]{2,1,0:T(8,128)(2,1)S(1)}, bf16[8,128,128]{2,1,0:T(8,128)(2,1)S(1)}, u32[]{:S(2)}, u32[]{:S(2)}) collective-permute-start(bf16[8,128,128]{2,1,0:T(8,128)(2,1)S(1)} %broadcast_select_fusion.3), channel_id=1, source_target_pairs={{0,4},{4,0},{8,12},{12,8},{16,20},{20,16},{24,28},{28,24},{1,5},{5... | collective-permute-start | bytes 786440 | tf_op jit(solution)/shard_map/ppermute | solution.py:273
  191.8 55.6 %copy-start.3 = (bf16[16,128,128]{2,1,0:T(8,128)(2,1)S(1)}, bf16[16,128,128]{2,1,0:T(8,128)(2,1)}, u32[]{:S(2)}) copy-start(bf16[16,128,128]{2,1,0:T(8,128)(2,1)} %shard_map.121) | copy-start | bytes 1572868
  251.6 33.8 %collective-permute-start.11 = (bf16[384,2048]{1,0:T(8,128)(2,1)}, bf16[384,2048]{1,0:T(8,128)(2,1)}, u32[]{:S(2)}, u32[]{:S(2)}) collective-permute-start(bf16[384,2048]{1,0:T(8,128)(2,1)} %slice.44), channel_id=1, source_target_pairs={{0,8},{8,16},{16,24},{24,28},{28,20},{20,12},{12,4},{4,0},{1,9},{9... | collective-permute-start | bytes 4718600 | tf_op jit(solution)/shard_map/ppermute | solution.py:225
  252.8 35.9 %collective-permute-start.12 = (bf16[384,2048]{1,0:T(8,128)(2,1)}, bf16[384,2048]{1,0:T(8,128)(2,1)}, u32[]{:S(2)}, u32[]{:S(2)}) collective-permute-start(bf16[384,2048]{1,0:T(8,128)(2,1)} %slice.45), channel_id=1, source_target_pairs={{8,0},{16,8},{24,16},{28,24},{20,28},{12,20},{4,12},{0,4},{9,1},{1... | collective-permute-start | bytes 4718600 | tf_op jit(solution)/shard_map/ppermute | solution.py:226
  267.1 4.1 %copy-start.1 = (f32[512,2048]{1,0:T(8,128)S(1)}, f32[512,2048]{1,0:T(8,128)}, u32[]{:S(2)}) copy-start(f32[512,2048]{1,0:T(8,128)} %add_add_fusion.1) | copy-start | bytes 12582916
  274.4 17.2 %copy-start.2 = (f32[512,2048]{1,0:T(8,128)S(1)}, f32[512,2048]{1,0:T(8,128)}, u32[]{:S(2)}) copy-start(f32[512,2048]{1,0:T(8,128)} %get-tuple-element.67.refs_4_) | copy-start | bytes 12582916
  274.4 17.2 %copy-start.12 = (f32[2048]{0:T(1024)S(1)}, f32[2048]{0:T(1024)}, u32[]{:S(2)}) copy-start(f32[2048]{0:T(1024)} %param.17) | copy-start | bytes 24580
  315.9 8.1 %collective-permute-start.13 = (bf16[8,128,128]{2,1,0:T(8,128)(2,1)S(1)}, bf16[8,128,128]{2,1,0:T(8,128)(2,1)S(1)}, u32[]{:S(2)}, u32[]{:S(2)}) collective-permute-start(bf16[8,128,128]{2,1,0:T(8,128)(2,1)S(1)} %constant_dynamic-slice_fusion), channel_id=1, source_target_pairs={{0,4},{4,0},{8,12},{12,8},{16,20},{20,16},{24,28},{28,24},{1,5},{5... | collective-permute-start | bytes 786440 | tf_op jit(solution)/shard_map/ppermute | solution.py:254
  325.1 18.8 %collective-permute-start.14 = (bf16[8,128,128]{2,1,0:T(8,128)(2,1)S(1)}, bf16[8,128,128]{2,1,0:T(8,128)(2,1)S(1)}, u32[]{:S(2)}, u32[]{:S(2)}) collective-permute-start(bf16[8,128,128]{2,1,0:T(8,128)(2,1)S(1)} %fusion.28), channel_id=1, source_target_pairs={{28,20},{24,16},{20,12},{16,8},{12,4},{8,0},{29,21},{25,17},{21,13... | collective-permute-start | bytes 786440 | tf_op jit(solution)/shard_map/ppermute | solution.py:264
  326.4 31.2 %collective-permute-start.15 = (bf16[8,128,128]{2,1,0:T(8,128)(2,1)S(1)}, bf16[8,128,128]{2,1,0:T(8,128)(2,1)S(1)}, u32[]{:S(2)}, u32[]{:S(2)}) collective-permute-start(bf16[8,128,128]{2,1,0:T(8,128)(2,1)S(1)} %fusion.28), channel_id=1, source_target_pairs={{28,12},{24,8},{20,4},{16,0},{29,13},{25,9},{21,5},{17,1},{30,14},... | collective-permute-start | bytes 786440 | tf_op jit(solution)/shard_map/ppermute | solution.py:264
  327.7 29.9 %collective-permute-start.16 = (bf16[8,128,128]{2,1,0:T(8,128)(2,1)S(1)}, bf16[8,128,128]{2,1,0:T(8,128)(2,1)S(1)}, u32[]{:S(2)}, u32[]{:S(2)}) collective-permute-start(bf16[8,128,128]{2,1,0:T(8,128)(2,1)S(1)} %fusion.28), channel_id=1, source_target_pairs={{28,4},{24,0},{29,5},{25,1},{30,6},{26,2},{31,7},{27,3}} | collective-permute-start | bytes 786440 | tf_op jit(solution)/shard_map/ppermute | solution.py:264
  329.0 28.6 %copy-start.8 = (bf16[16,128,128]{2,1,0:T(8,128)(2,1)S(1)}, bf16[16,128,128]{2,1,0:T(8,128)(2,1)}, u32[]{:S(2)}) copy-start(bf16[16,128,128]{2,1,0:T(8,128)(2,1)} %get-tuple-element.68) | copy-start | bytes 1572868
  358.0 6.4 %collective-permute-start.17 = (bf16[8,128,128]{2,1,0:T(8,128)(2,1)S(1)}, bf16[8,128,128]{2,1,0:T(8,128)(2,1)S(1)}, u32[]{:S(2)}, u32[]{:S(2)}) collective-permute-start(bf16[8,128,128]{2,1,0:T(8,128)(2,1)S(1)} %broadcast_select_fusion.7), channel_id=1, source_target_pairs={{0,4},{4,0},{8,12},{12,8},{16,20},{20,16},{24,28},{28,24},{1,5},{5... | collective-permute-start | bytes 786440 | tf_op jit(solution)/shard_map/ppermute | solution.py:273
  (2 other events, 3.3 us)
Sparse Core Ops, SparseCore 0:
  9.6 49.0 all-gather.2

commit v4 on v3

--- a/solution.py
+++ b/solution.py
@@ -226,9 +226,13 @@
         new_right = lax.ppermute(right[half:] if last else right, "ctx", down)
         total = total + term(left, -step, 0)
         total = total + term(right, step, 0)
-        left, right, total, result = lax.optimization_barrier(
-            (new_left, new_right, total, result)
-        )
+        if last:
+            left, right, total, result = lax.optimization_barrier(
+                (new_left, new_right, total, result)
+            )
+        else:
+            left, right = new_left, new_right
+            total, result = lax.optimization_barrier((total, result))
     total = total + term(left, -(count // 2), 0)
     total = total + term(right, count // 2, half)
     return total, result
@@ -259,13 +263,29 @@
     pair = pair.astype(jnp.bfloat16)
     last = marks[jnp.maximum(2 * high - 1, 0)]
     into_first = jnp.zeros(pair.shape, f32)
-    hops = range(1, count // 2)
-    moves = [[(index(i), index(i + 2 * hop)) for i in range(count - 2 * hop)] for hop in hops]
-    arrived = yield [lax.ppermute(pair, "ctx", move) for move in moves]
-    for hop, came in zip(hops, arrived):
+
+    def along(state, hop):
+        moves = [(index(i), index(i + 2 * hop)) for i in range(count - 2 * hop)]
+        return lax.ppermute(state, "ctx", moves)
+
+    def reached(hop, mark):
         from_high = high - hop
-        same = (from_high >= 0) & (marks[jnp.maximum(2 * from_high + 1, 0)] == last)
-        into_first = into_first + fade(rate, 2 * (hop - 1), same) * came.astype(f32)
+        return (from_high >= 0) & (marks[jnp.maximum(2 * from_high + 1, 0)] == mark)
+
+    if reverse:
+        hop = 1
+        while hop < count // 2:
+            came = yield along(pair, hop)
+            came = came.astype(f32)
+            into_first += fade(rate, 2 * (hop - 1), reached(hop, last)) * came
+            covered = fade(rate, 2 * hop, reached(hop, marks[2 * high + 1])) * came
+            pair = (pair.astype(f32) + covered).astype(jnp.bfloat16)
+            hop *= 2
+    else:
+        hops = range(1, count // 2)
+        arrived = yield [along(pair, hop) for hop in hops]
+        for hop, came in zip(hops, arrived):
+            into_first += fade(rate, 2 * (hop - 1), reached(hop, last)) * came.astype(f32)
     same = (high > 0) & (marks[2 * high] == last)
     into_second = first + fade(rate, 1, same) * into_first
     into_first, into_second = into_first.astype(jnp.bfloat16), into_second.astype(jnp.bfloat16)
@@ -277,7 +297,8 @@
 
 def finish_exchange(steps, arrived):
     try:
-        steps.send(arrived)
+        while True:
+            arrived = steps.send(arrived)
     except StopIteration as end:
         return end.value
 
@@ -356,6 +377,7 @@
     )
     steps = exchange(total, starts, slopes, tokens, True)
     arrived = steps.send(next(steps))
+    arrived = steps.send(arrived)
     dq, dk, dv = call(
         backward_kernel, heads,
         [smem(), col, col, col, col, stack(blocks), table_spec, *seg_specs],
@@ -364,7 +386,7 @@
         6 * unit, 10 * size,
     )
     arrived, dq, dk, dv = lax.optimization_barrier((arrived, dq, dk, dv))
-    leaving = finish_exchange(steps, steps.send(arrived))
+    leaving = finish_exchange(steps, arrived)
     dk, dv = call(
         finish_kernel, heads,
         [smem(), smem(), one_state(), col, col, stack(blocks), table_spec, col, col],

time: 385 us -> 377 us (0.979)
    ppermute x3, waiting for transfers between devices: 11 us -> 67.6 us  [ring_matmul(): new_left = lax.ppermute(left[:half] if last else left, 'ctx', up)]
    ppermute x2, waiting for transfers between devices: 56.1 us -> 6.06 us  [exchange(): lax.ppermute(jnp.where(low == 0, into_second, into_first), 'ctx', swap)]
    ppermute x6 -> x5, waiting for transfers between devices: 50.8 us -> 44.6 us  [along(): return lax.ppermute(state, 'ctx', moves)]
    ppermute x6 -> x5, starting transfers between devices: 16.1 us -> 14.2 us  [along(): return lax.ppermute(state, 'ctx', moves)]
  transfers between devices with their start and end apart: 19 -> 18, of which waited for: 10 -> 8; matrix products, arithmetic and copies ran while one was open for 12% -> 14% of each run, Pallas kernels for 9% -> 9%
where the time goes in v4:
time: 377 us; the launch traced here: 375 us
  waiting for transfers between devices  177 us (47%)
  Pallas kernels  55.2 us (15%)
  between operations  38.8 us (10%)
  matrix products  37.4 us (10%)
  starting transfers between devices  33.6 us (9%)
  other arithmetic  14.2 us (4%)
  local copies, waits for them, and re-layouts  14 us (4%)
  blocking collectives  5.63 us (1%)
    ppermute x3, waiting for transfers between devices, ring_matmul(): new_left = lax.ppermute(left[:half] if last else left, 'ctx', up)  67.6 us
    ppermute x2, waiting for transfers between devices, exchange(): other = (yield lax.ppermute(part(local, 1 - low), 'ctx', swap))  57.6 us
    pallas_call x5, Pallas kernels, call(): pl.pallas_call(step, grid=(heads // PER,), in_specs=[spec for _, spec in...  55.2 us
    ppermute x5, waiting for transfers between devices, along(): return lax.ppermute(state, 'ctx', moves)  44.6 us
    dot_general x9, matrix products, term(): return jnp.dot(part, block, preferred_element_type=jnp.float32)  37.4 us
    ppermute x5, starting transfers between devices, along(): return lax.ppermute(state, 'ctx', moves)  14.2 us
  transfers between devices with their start and end apart: 18, of which 8 were waited for; matrix products, arithmetic and copies ran while one was open for 14% of the time, Pallas kernels for 9%

profile of v4, /device:TPU:0, one launch (start us, length us, event | category | flops | bytes accessed | tf_op | source)
XLA Modules:
  0.0 375.4 jit_solution(9189059522991187081)
XLA Ops:
  7.9 3.1 collective-permute-start
  13.4 2.0 fusion.54
  16.8 2.0 and_convert_fusion.4
  19.4 7.8 %shard_map.121 = bf16[16,128,128]{2,1,0:T(8,128)(2,1)} custom-call(f32[16]{0:T(128)} %refs_0_.9, f32[3,2]{1,0:T(4,128)} %pad_maximum_fusion.2.refs_1_, bf16[512,2048]{1,0:T(8,128)(2,1)} %refs_3_.7, bf16[512,2048]{1,0:T(8,128)(2,1)} %refs_4_.3, f32[512,6]{1,0:T(8,128)} %copy.34.refs_4_.refs_6_), custom_call_target="tpu_custom_call" | custom-call | flops 268435456 | bytes 4194304 | tf_op jit(solution)/shard_map/pallas_call | solution.py:183
  28.2 2.0 collective-permute-start.2
  30.2 54.6 %collective-permute-done.2 = bf16[8,128,128]{2,1,0:T(8,128)(2,1)S(1)} collective-permute-done((bf16[8,128,128]{2,1,0:T(8,128)(2,1)S(1)}, bf16[8,128,128]{2,1,0:T(8,128)(2,1)S(1)}, u32[]{:S(2)}, u32[]{:S(2)}) %collective-permute-start.2) | collective-permute-done | bytes 262176 | tf_op jit(solution)/shard_map/ppermute | solution.py:258
  84.9 2.0 collective-permute-start.6
  86.9 67.6 %collective-permute-done.3 = bf16[768,2048]{1,0:T(8,128)(2,1)} collective-permute-done((bf16[768,2048]{1,0:T(8,128)(2,1)}, bf16[768,2048]{1,0:T(8,128)(2,1)}, u32[]{:S(2)}, u32[]{:S(2)}) %collective-permute-start.3) | collective-permute-done | bytes 3145760 | tf_op jit(solution)/shard_map/ppermute | solution.py:225
  181.8 5.6 %collective-permute-start.10 = (bf16[8,128,128]{2,1,0:T(8,128)(2,1)}, bf16[8,128,128]{2,1,0:T(8,128)(2,1)}, u32[]{:S(2)}, u32[]{:S(2)}) collective-permute-start(bf16[8,128,128]{2,1,0:T(8,128)(2,1)} %fusion.25), channel_id=1, source_target_pairs={{0,16},{4,20},{8,24},{12,28},{1,17},{5,21},{9,25},{13,29},{2,18},{... | collective-permute-start | bytes 786440 | tf_op jit(solution)/shard_map/ppermute | solution.py:269
  187.4 2.8 collective-permute-start.11
  190.2 3.2 collective-permute-start.9
  193.5 4.1 %fusion.13 = f32[512,2048]{1,0:T(8,128)S(1)} fusion(bf16[768,2048]{1,0:T(8,128)(2,1)} %collective-permute-done, bf16[4,512,1536]{2,1,0:T(8,128)(2,1)} %bitcast.122, s32[]{:T(128)S(6)} %select_n.305, s32[]{:T(128)S(6)} %select_n.306), kind=kOutput, calls=%fused_computation.15 | convolution fusion | flops 1610612736 | bytes 8126472 | tf_op jit(solution)/shard_map/dot_general | solution.py:213
  202.1 27.2 %collective-permute-done.10 = bf16[8,128,128]{2,1,0:T(8,128)(2,1)} collective-permute-done((bf16[8,128,128]{2,1,0:T(8,128)(2,1)}, bf16[8,128,128]{2,1,0:T(8,128)(2,1)}, u32[]{:S(2)}, u32[]{:S(2)}) %collective-permute-start.10) | collective-permute-done | bytes 262176 | tf_op jit(solution)/shard_map/ppermute | solution.py:269
  229.3 5.6 %collective-permute-done.11 = bf16[8,128,128]{2,1,0:T(8,128)(2,1)} collective-permute-done((bf16[8,128,128]{2,1,0:T(8,128)(2,1)}, bf16[8,128,128]{2,1,0:T(8,128)(2,1)}, u32[]{:S(2)}, u32[]{:S(2)}) %collective-permute-start.11) | collective-permute-done | bytes 262176 | tf_op jit(solution)/shard_map/ppermute | solution.py:269
  235.0 3.2 collective-permute-done.9
  239.7 2.5 collective-permute-start.12
  242.1 2.7 slice.46
  244.9 7.0 %collective-permute-start.5 = (bf16[384,2048]{1,0:T(8,128)(2,1)}, bf16[384,2048]{1,0:T(8,128)(2,1)}, u32[]{:S(2)}, u32[]{:S(2)}) collective-permute-start(bf16[384,2048]{1,0:T(8,128)(2,1)} %slice.46), channel_id=1, source_target_pairs={{0,8},{8,16},{16,24},{24,28},{28,20},{20,12},{12,4},{4,0},{1,9},{9... | collective-permute-start | bytes 4718600 | tf_op jit(solution)/shard_map/ppermute | solution.py:225
  253.2 3.8 %fusion.10 = f32[512,2048]{1,0:T(8,128)S(1)} fusion(bf16[768,2048]{1,0:T(8,128)(2,1)} %collective-permute-done.3, bf16[4,512,1536]{2,1,0:T(8,128)(2,1)S(1)} %bitcast.128, s32[]{:T(128)S(6)} %select_n.323, s32[]{:T(128)S(6)} %select_n.324), kind=kOutput, calls=%fused_computation.12 | convolution fusion | flops 1610612736 | bytes 8126472 | tf_op jit(solution)/shard_map/dot_general | solution.py:213
  257.0 5.8 %add_add_fusion.1 = f32[512,2048]{1,0:T(8,128)} fusion(f32[512,2048]{1,0:T(8,128)S(1)} %add_add_fusion.2, f32[512,2048]{1,0:T(8,128)S(1)} %fusion.10, bf16[768,2048]{1,0:T(8,128)(2,1)} %collective-permute-done.6, bf16[4,512,1536]{2,1,0:T(8,128)(2,1)S(1)} %bitcast.129, s32[]{:T(128)S(6)} %select_n.327, s32[]{:T(128)S(6)} %select_n.328), kind=kOutput, calls=%fused_computation.4 | convolution fusion | flops 1612709888 | bytes 16515080 | tf_op jit(solution)/shard_map/dot_general | solution.py:213
  262.8 5.7 %fusion.4 = f32[512,2048]{1,0:T(8,128)} fusion(bf16[768,2048]{1,0:T(8,128)(2,1)} %collective-permute-done.4, bf16[4,512,1536]{2,1,0:T(8,128)(2,1)S(1)} %bitcast.130, s32[]{:T(128)S(6)} %select_n.340, s32[]{:T(128)S(6)} %select_n.341), kind=kOutput, calls=%fused_computation.8 | convolution fusion | flops 1610612736 | bytes 8126472 | tf_op jit(solution)/shard_map/dot_general | solution.py:213
  270.9 11.4 %shard_map.122 = (f32[512,2048]{1,0:T(8,128)}, bf16[2,16,128,128]{3,2,1,0:T(8,128)(2,1)}) custom-call(f32[16]{0:T(128)} %refs_0_.9, f32[3,2]{1,0:T(4,128)} %pad_maximum_fusion.2.refs_1_, bf16[16,128,128]{2,1,0:T(8,128)(2,1)} %pad_maximum_fusion.refs_2_, bf16[512,2048]{1,0:T(8,128)(2,1)} %refs_1_.1, bf16[512,2048]{1,0:T(8,128)(2,1)} %refs_3_.7, ...), custom_call_target="tpu_custom_call" | custom-call | flops 1610612736 | bytes 12582912 | tf_op jit(solution)/shard_map/pallas_call | solution.py:183
  282.3 5.6 %add_add_fusion = f32[512,2048]{1,0:T(8,128)S(1)} fusion(f32[512,2048]{1,0:T(8,128)} %add_add_fusion.1, f32[512,2048]{1,0:T(8,128)} %fusion.4, bf16[768,2048]{1,0:T(8,128)(2,1)S(1)} %collective-permute-done.7, bf16[4,512,1536]{2,1,0:T(8,128)(2,1)} %bitcast.123, s32[]{:T(128)S(6)} %select_n.344, s32[]{:T(128)S(6)} %select_n.345), kind=kOutput, calls=%fused_computation.3 | convolution fusion | flops 1612709888 | bytes 16515080 | tf_op jit(solution)/shard_map/dot_general | solution.py:213
  288.0 3.0 fusion.38
  291.0 5.6 %multiply_reduce_fusion = (f32[512]{0:T(512)S(1)}, f32[512]{0:T(512)S(1)}, f32[512,2048]{1,0:T(8,128)}) fusion(f32[512,2048]{1,0:T(8,128)S(1)} %copy-done, bf16[384,2048]{1,0:T(8,128)(2,1)} %collective-permute-done.8, bf16[4,512,1536]{2,1,0:T(8,128)(2,1)} %bitcast.125, s32[]{:T(128)S(6)} %select_n.355, s32[]{:T(128)S(6)} %select_n.356, ...), kind=kOutput, calls=%fused_computation | convolution fusion | flops 812645376 | bytes 18755592 | tf_op jit(solution)/shard_map/dot_general | solution.py:213
  296.6 5.6 %all-reduce = (f32[512]{0:T(512)S(1)}, f32[512]{0:T(512)S(1)}) all-reduce(f32[512]{0:T(512)S(1)} %get-tuple-element.72, f32[512]{0:T(512)S(1)} %get-tuple-element.71), channel_id=1, replica_groups=mesh['ctx'=8,'head'=4] {'head'}, use_global_device_ids=true, to_apply=%region_4.5 | all-reduce | flops 1024 | bytes 8192 | tf_op jit(solution)/shard_map/psum | solution.py:366
  303.1 11.2 %shard_map.123 = (bf16[512,2048]{1,0:T(8,128)(2,1)}, f32[2,16,128,128]{3,2,1,0:T(8,128)}, bf16[16,128,128]{2,1,0:T(8,128)(2,1)}) custom-call(f32[16]{0:T(128)} %refs_0_.9, f32[3,2]{1,0:T(4,128)} %pad_maximum_fusion.2.refs_1_, bf16[512,2048]{1,0:T(8,128)(2,1)} %refs_1_.1, f32[512,2048]{1,0:T(8,128)} %get-tuple-element.132.refs_3_, ...), custom_call_target="tpu_custom_call" | custom-call | flops 268435456 | bytes 14680064 | tf_op jit(solution)/shard_map/pallas_call | solution.py:183
  320.4 3.0 collective-permute-done.13
  325.8 8.5 %collective-permute-done.14 = bf16[8,128,128]{2,1,0:T(8,128)(2,1)S(1)} collective-permute-done((bf16[8,128,128]{2,1,0:T(8,128)(2,1)S(1)}, bf16[8,128,128]{2,1,0:T(8,128)(2,1)S(1)}, u32[]{:S(2)}, u32[]{:S(2)}) %collective-permute-start.14) | collective-permute-done | bytes 262176 | tf_op jit(solution)/shard_map/ppermute | solution.py:269
  335.8 14.8 %shard_map.124 = (bf16[512,2048]{1,0:T(8,128)(2,1)}, f32[512,2048]{1,0:T(8,128)}, f32[512,2048]{1,0:T(8,128)}) custom-call(f32[16]{0:T(128)} %refs_0_.9, bf16[512,2048]{1,0:T(8,128)(2,1)} %refs_1_.1, bf16[512,2048]{1,0:T(8,128)(2,1)} %refs_3_.7, bf16[512,2048]{1,0:T(8,128)(2,1)} %refs_4_.3, bf16[512,2048]{1,0:T(8,128)(2,1)} %get-tuple-element.59.refs_4_, ...), custom_call_target="tpu_custom_call" | custom-call | flops 3221225472 | bytes 20971520 | tf_op jit(solution)/shard_map/pallas_call | solution.py:183
  351.5 6.1 %collective-permute-done.16 = bf16[8,128,128]{2,1,0:T(8,128)(2,1)S(1)} collective-permute-done((bf16[8,128,128]{2,1,0:T(8,128)(2,1)S(1)}, bf16[8,128,128]{2,1,0:T(8,128)(2,1)S(1)}, u32[]{:S(2)}, u32[]{:S(2)}) %collective-permute-start.16) | collective-permute-done | bytes 262176 | tf_op jit(solution)/shard_map/ppermute | solution.py:293
  358.5 10.0 %shard_map.125 = (bf16[512,2048]{1,0:T(8,128)(2,1)}, bf16[512,2048]{1,0:T(8,128)(2,1)}) custom-call(f32[16]{0:T(128)} %refs_0_.9, f32[3,2]{1,0:T(4,128)} %pad_maximum_fusion.2.refs_1_, bf16[16,128,128]{2,1,0:T(8,128)(2,1)} %pad_maximum_fusion.1.refs_2_, bf16[512,2048]{1,0:T(8,128)(2,1)} %refs_3_.7, bf16[512,2048]{1,0:T(8,128)(2,1)} %refs_4_.3, ...), custom_call_target="tpu_custom_call" | custom-call | flops 536870912 | bytes 20971520 | tf_op jit(solution)/shard_map/pallas_call | solution.py:183
  (99 shorter events, 31.3 us)
Async XLA Ops:
  7.2 149.4 %copy-start.11 = (s32[8]{0:T(128)S(1)}, s32[8]{0:T(128)}, u32[]{:S(2)}) copy-start(s32[8]{0:T(128)} %constant.258.clone) | copy-start | bytes 100
  7.2 155.9 %copy-start.6 = (s32[8]{0:T(128)S(1)}, s32[8]{0:T(128)}, u32[]{:S(2)}) copy-start(s32[8]{0:T(128)} %constant.257.clone) | copy-start | bytes 100
  7.2 172.8 %copy-start.7 = (f32[16]{0:T(128)S(1)}, f32[16]{0:T(128)}, u32[]{:S(2)}) copy-start(f32[16]{0:T(128)} %refs_0_.9) | copy-start | bytes 196
  7.2 186.2 %all-gather.3.cloned.1.call-start = ((), (), s32[]{:S(2)}) async-start(), calls=%async_computation | async-start | bytes 7864320 | tf_op jit(solution)/shard_map/all_gather | solution.py:364
  7.9 76.9 %collective-permute-start = (bf16[768,2048]{1,0:T(8,128)(2,1)}, bf16[768,2048]{1,0:T(8,128)(2,1)}, u32[]{:S(2)}, u32[]{:S(2)}) collective-permute-start(bf16[768,2048]{1,0:T(8,128)(2,1)} %param.16), channel_id=1, source_target_pairs={{0,8},{8,16},{16,24},{24,28},{28,20},{20,12},{12,4},{4,0},{1,9},{9... | collective-permute-start | bytes 9437192 | tf_op jit(solution)/shard_map/ppermute | solution.py:218
  11.0 73.9 %collective-permute-start.1 = (bf16[768,2048]{1,0:T(8,128)(2,1)}, bf16[768,2048]{1,0:T(8,128)(2,1)S(1)}, u32[]{:S(2)}, u32[]{:S(2)}) collective-permute-start(bf16[768,2048]{1,0:T(8,128)(2,1)} %param.16), channel_id=1, source_target_pairs={{8,0},{16,8},{24,16},{28,24},{20,28},{12,20},{4,12},{0,4},{9,1},{1... | collective-permute-start | bytes 9437192 | tf_op jit(solution)/shard_map/ppermute | solution.py:219
  12.0 185.6 %copy-start.8 = (s32[512]{0:T(512)}, s32[512]{0:T(512)S(1)}, u32[]{:S(2)}) copy-start(s32[512]{0:T(512)S(1)} %slice.37) | copy-start | bytes 6148
  28.2 56.6 %collective-permute-start.2 = (bf16[8,128,128]{2,1,0:T(8,128)(2,1)S(1)}, bf16[8,128,128]{2,1,0:T(8,128)(2,1)S(1)}, u32[]{:S(2)}, u32[]{:S(2)}) collective-permute-start(bf16[8,128,128]{2,1,0:T(8,128)(2,1)S(1)} %constant_dynamic-slice_fusion.1), channel_id=1, source_target_pairs={{0,4},{4,0},{8,12},{12,8},{16,20},{20,16},{24,28},{28,24},{1,5},{5... | collective-permute-start | bytes 786440 | tf_op jit(solution)/shard_map/ppermute | solution.py:258
  84.9 69.9 %copy-start.2 = (bf16[768,2048]{1,0:T(8,128)(2,1)}, bf16[768,2048]{1,0:T(8,128)(2,1)S(1)}, u32[]{:S(2)}) copy-start(bf16[768,2048]{1,0:T(8,128)(2,1)S(1)} %collective-permute-done.1) | copy-start | bytes 9437188
  84.9 69.7 %collective-permute-start.3 = (bf16[768,2048]{1,0:T(8,128)(2,1)}, bf16[768,2048]{1,0:T(8,128)(2,1)}, u32[]{:S(2)}, u32[]{:S(2)}) collective-permute-start(bf16[768,2048]{1,0:T(8,128)(2,1)} %collective-permute-done), channel_id=1, source_target_pairs={{0,8},{8,16},{16,24},{24,28},{28,20},{20,12},{12,4},{4,0},{1,9},{9... | collective-permute-start | bytes 9437192 | tf_op jit(solution)/shard_map/ppermute | solution.py:225
  84.9 69.9 %collective-permute-start.6 = (bf16[768,2048]{1,0:T(8,128)(2,1)S(1)}, bf16[768,2048]{1,0:T(8,128)(2,1)}, u32[]{:S(2)}, u32[]{:S(2)}) collective-permute-start(bf16[768,2048]{1,0:T(8,128)(2,1)S(1)} %collective-permute-done.1), channel_id=1, source_target_pairs={{8,0},{16,8},{24,16},{28,24},{20,28},{12,20},{4,12},{0,4},{9,1},{1... | collective-permute-start | bytes 9437192 | tf_op jit(solution)/shard_map/ppermute | solution.py:226
  154.5 87.6 %collective-permute-start.4 = (bf16[768,2048]{1,0:T(8,128)(2,1)}, bf16[768,2048]{1,0:T(8,128)(2,1)}, u32[]{:S(2)}, u32[]{:S(2)}) collective-permute-start(bf16[768,2048]{1,0:T(8,128)(2,1)} %collective-permute-done.3), channel_id=1, source_target_pairs={{0,8},{8,16},{16,24},{24,28},{28,20},{20,12},{12,4},{4,0},{1,9},{9... | collective-permute-start | bytes 9437192 | tf_op jit(solution)/shard_map/ppermute | solution.py:225
  154.8 97.1 %collective-permute-start.7 = (bf16[768,2048]{1,0:T(8,128)(2,1)}, bf16[768,2048]{1,0:T(8,128)(2,1)S(1)}, u32[]{:S(2)}, u32[]{:S(2)}) collective-permute-start(bf16[768,2048]{1,0:T(8,128)(2,1)} %collective-permute-done.6), channel_id=1, source_target_pairs={{8,0},{16,8},{24,16},{28,24},{20,28},{12,20},{4,12},{0,4},{9,1},{1... | collective-permute-start | bytes 9437192 | tf_op jit(solution)/shard_map/ppermute | solution.py:226
  181.8 47.5 %collective-permute-start.10 = (bf16[8,128,128]{2,1,0:T(8,128)(2,1)}, bf16[8,128,128]{2,1,0:T(8,128)(2,1)}, u32[]{:S(2)}, u32[]{:S(2)}) collective-permute-start(bf16[8,128,128]{2,1,0:T(8,128)(2,1)} %fusion.25), channel_id=1, source_target_pairs={{0,16},{4,20},{8,24},{12,28},{1,17},{5,21},{9,25},{13,29},{2,18},{... | collective-permute-start | bytes 786440 | tf_op jit(solution)/shard_map/ppermute | solution.py:269
  187.4 47.5 %collective-permute-start.11 = (bf16[8,128,128]{2,1,0:T(8,128)(2,1)}, bf16[8,128,128]{2,1,0:T(8,128)(2,1)}, u32[]{:S(2)}, u32[]{:S(2)}) collective-permute-start(bf16[8,128,128]{2,1,0:T(8,128)(2,1)} %fusion.25), channel_id=1, source_target_pairs={{0,24},{4,28},{1,25},{5,29},{2,26},{6,30},{3,27},{7,31}} | collective-permute-start | bytes 786440 | tf_op jit(solution)/shard_map/ppermute | solution.py:269
  190.2 48.0 %collective-permute-start.9 = (bf16[8,128,128]{2,1,0:T(8,128)(2,1)}, bf16[8,128,128]{2,1,0:T(8,128)(2,1)}, u32[]{:S(2)}, u32[]{:S(2)}) collective-permute-start(bf16[8,128,128]{2,1,0:T(8,128)(2,1)} %fusion.25), channel_id=1, source_target_pairs={{0,8},{4,12},{8,16},{12,20},{16,24},{20,28},{1,9},{5,13},{9,17},{1... | collective-permute-start | bytes 786440 | tf_op jit(solution)/shard_map/ppermute | solution.py:269
  193.4 4.1 %copy-start.4 = (bf16[2048,1536]{1,0:T(8,128)(2,1)S(1)}, bf16[2048,1536]{1,0:T(8,128)(2,1)}, u32[]{:S(2)}) copy-start(bf16[2048,1536]{1,0:T(8,128)(2,1)} %all-gather.3.cloned.1.call-done) | copy-start | bytes 18874372
  193.4 4.9 %copy-start.10 = (bf16[768,2048]{1,0:T(8,128)(2,1)S(1)}, bf16[768,2048]{1,0:T(8,128)(2,1)}, u32[]{:S(2)}) copy-start(bf16[768,2048]{1,0:T(8,128)(2,1)} %param.16) | copy-start | bytes 9437188
  198.3 1.9 copy-start.3
  200.2 38.0 %copy-start.1 = (bf16[16,128,128]{2,1,0:T(8,128)(2,1)S(1)}, bf16[16,128,128]{2,1,0:T(8,128)(2,1)}, u32[]{:S(2)}) copy-start(bf16[16,128,128]{2,1,0:T(8,128)(2,1)} %shard_map.121) | copy-start | bytes 1572868
  239.7 28.9 %collective-permute-start.12 = (bf16[8,128,128]{2,1,0:T(8,128)(2,1)S(1)}, bf16[8,128,128]{2,1,0:T(8,128)(2,1)S(1)}, u32[]{:S(2)}, u32[]{:S(2)}) collective-permute-start(bf16[8,128,128]{2,1,0:T(8,128)(2,1)S(1)} %broadcast_select_fusion.3), channel_id=1, source_target_pairs={{0,4},{4,0},{8,12},{12,8},{16,20},{20,16},{24,28},{28,24},{1,5},{5... | collective-permute-start | bytes 786440 | tf_op jit(solution)/shard_map/ppermute | solution.py:293
  244.9 43.1 %collective-permute-start.5 = (bf16[384,2048]{1,0:T(8,128)(2,1)}, bf16[384,2048]{1,0:T(8,128)(2,1)}, u32[]{:S(2)}, u32[]{:S(2)}) collective-permute-start(bf16[384,2048]{1,0:T(8,128)(2,1)} %slice.46), channel_id=1, source_target_pairs={{0,8},{8,16},{16,24},{24,28},{28,20},{20,12},{12,4},{4,0},{1,9},{9... | collective-permute-start | bytes 4718600 | tf_op jit(solution)/shard_map/ppermute | solution.py:225
  253.2 34.7 %collective-permute-start.8 = (bf16[384,2048]{1,0:T(8,128)(2,1)}, bf16[384,2048]{1,0:T(8,128)(2,1)}, u32[]{:S(2)}, u32[]{:S(2)}) collective-permute-start(bf16[384,2048]{1,0:T(8,128)(2,1)} %slice.47), channel_id=1, source_target_pairs={{8,0},{16,8},{24,16},{28,24},{20,28},{12,20},{4,12},{0,4},{9,1},{1... | collective-permute-start | bytes 4718600 | tf_op jit(solution)/shard_map/ppermute | solution.py:226
  287.9 3.1 copy-start
  287.9 3.1 copy-start.9
  315.3 8.1 %collective-permute-start.13 = (bf16[8,128,128]{2,1,0:T(8,128)(2,1)S(1)}, bf16[8,128,128]{2,1,0:T(8,128)(2,1)S(1)}, u32[]{:S(2)}, u32[]{:S(2)}) collective-permute-start(bf16[8,128,128]{2,1,0:T(8,128)(2,1)S(1)} %constant_dynamic-slice_fusion), channel_id=1, source_target_pairs={{0,4},{4,0},{8,12},{12,8},{16,20},{20,16},{24,28},{28,24},{1,5},{5... | collective-permute-start | bytes 786440 | tf_op jit(solution)/shard_map/ppermute | solution.py:258
  324.5 9.8 %collective-permute-start.14 = (bf16[8,128,128]{2,1,0:T(8,128)(2,1)S(1)}, bf16[8,128,128]{2,1,0:T(8,128)(2,1)S(1)}, u32[]{:S(2)}, u32[]{:S(2)}) collective-permute-start(bf16[8,128,128]{2,1,0:T(8,128)(2,1)S(1)} %fusion.28), channel_id=1, source_target_pairs={{28,20},{24,16},{20,12},{16,8},{12,4},{8,0},{29,21},{25,17},{21,13... | collective-permute-start | bytes 786440 | tf_op jit(solution)/shard_map/ppermute | solution.py:269
  334.5 16.1 %collective-permute-start.15 = (bf16[8,128,128]{2,1,0:T(8,128)(2,1)S(1)}, bf16[8,128,128]{2,1,0:T(8,128)(2,1)S(1)}, u32[]{:S(2)}, u32[]{:S(2)}) collective-permute-start(bf16[8,128,128]{2,1,0:T(8,128)(2,1)S(1)} %fusion.31), channel_id=1, source_target_pairs={{28,12},{24,8},{20,4},{16,0},{29,13},{25,9},{21,5},{17,1},{30,14},... | collective-permute-start | bytes 786440 | tf_op jit(solution)/shard_map/ppermute | solution.py:269
  335.8 14.9 %copy-start.5 = (bf16[16,128,128]{2,1,0:T(8,128)(2,1)S(1)}, bf16[16,128,128]{2,1,0:T(8,128)(2,1)}, u32[]{:S(2)}) copy-start(bf16[16,128,128]{2,1,0:T(8,128)(2,1)} %get-tuple-element.58) | copy-start | bytes 1572868
  350.9 6.6 %collective-permute-start.16 = (bf16[8,128,128]{2,1,0:T(8,128)(2,1)S(1)}, bf16[8,128,128]{2,1,0:T(8,128)(2,1)S(1)}, u32[]{:S(2)}, u32[]{:S(2)}) collective-permute-start(bf16[8,128,128]{2,1,0:T(8,128)(2,1)S(1)} %get-tuple-element.77), channel_id=1, source_target_pairs={{0,4},{4,0},{8,12},{12,8},{16,20},{20,16},{24,28},{28,24},{1,5},{5... | collective-permute-start | bytes 786440 | tf_op jit(solution)/shard_map/ppermute | solution.py:293
Sparse Core Ops, SparseCore 0:
  9.6 49.0 all-gather.2
